TPU v7x, 32 devices: a whole 2x2x4 slice. The times are simulated.
32 devices in a mesh: replica: 4 (over z), fsdp: 8 (over y, x, core).
Axes of the slice: x: 2, y: 2, z: 4, core: 2. Of those that a mesh axis runs over, the one named last changes fastest.
Arguments:
- tokens: bfloat16 [8192, 768], P(('replica', 'fsdp')), may hold values from -6 to 6
- seq_lengths: int32 [32, 2], P(('replica', 'fsdp')), may hold values from 1 to 255, as said below
- norm1_gain: bfloat16 [768], P('fsdp'), may hold values from 0.5 to 1.5
- qkv_weight: bfloat16 [768, 2304], P('fsdp'), may hold values from -0.21875 to 0.21875
- out_weight: bfloat16 [768, 768], P('fsdp'), may hold values from -0.875 to 0.875
- norm2_gain: bfloat16 [768], P('fsdp'), may hold values from 0.5 to 1.5
- in_weight: bfloat16 [768, 2304], P('fsdp'), may hold values from -0.21875 to 0.21875
- down_weight: bfloat16 [1152, 768], P(None, 'fsdp'), may hold values from -0.1875 to 0.1875
- cotangent: float32 [8192, 768], P(('replica', 'fsdp')), may hold values from -6 to 6
Outputs:
- output: bfloat16 [8192, 768], P(('replica', 'fsdp'))
- grad_tokens: float32 [8192, 768], P(('replica', 'fsdp'))
- grad_norm1: float32 [768], P('fsdp')
- grad_qkv: float32 [768, 2304], P('fsdp')
- grad_out: float32 [768, 768], P('fsdp')
- grad_norm2: float32 [768], P('fsdp')
- grad_in: float32 [768, 2304], P('fsdp')
- grad_down: float32 [1152, 768], P(None, 'fsdp')
Inputs may be any that keep to these rules, and one draw needn't show every extreme that they name: `seq_lengths`: row r holds the lengths of the two sequences packed first into device r's 256 slots; the two sum to 128 or more and to 256 at most, and in every draw some device's two sum to exactly 256.
All inputs are finite; a program needn't handle non-finite values.
Results may differ from a plain program's by a relative error of at most 0.02.
Values may be sent and summed in bfloat16 or wider, within the bound.
No kernel may reach another device: no remote copies, remote signals or barrier semaphores. Data moves between devices by JAX's collectives and lax.ppermute only.
A program may use at most 128 MiB of HBM per device.

v0:
```python
import jax
import jax.numpy as jnp
from jax import lax
from jax.sharding import PartitionSpec as P

HEAD = 64


NORM_EPS = 1e-05
ROPE_BASE = 160000.0
MASK_FILL = -1000000000.0


def slot_layout(length_pairs, slot_count):
    slot_index = jnp.arange(slot_count, dtype=jnp.int32)[None, :]
    first_length = length_pairs[:, 0:1]
    both_lengths = first_length + length_pairs[:, 1:2]
    segment = jnp.where(
        slot_index < first_length, 0, jnp.where(slot_index < both_lengths, 1, 2)
    ).astype(jnp.int32)
    begin = jnp.where(segment == 0, 0, jnp.where(segment == 1, first_length, both_lengths))
    return (segment, slot_index - begin)


def rope_tables(positions, head_size):
    half_size = head_size // 2
    frequency = ROPE_BASE ** (-(jnp.arange(half_size, dtype=jnp.float32) * 2.0) / head_size)
    angles = positions.astype(jnp.float32)[:, None] * frequency[None, :]
    return (jnp.cos(angles), jnp.sin(angles))


def rotate(values, cosine_table, sine_table):
    half_size = values.shape[-1] // 2
    first_half = values[..., :half_size]
    second_half = values[..., half_size:]
    cos_rows = cosine_table[:, None, :]
    sin_rows = sine_table[:, None, :]
    return jnp.concatenate(
        [
            first_half * cos_rows - second_half * sin_rows,
            second_half * cos_rows + first_half * sin_rows,
        ],
        -1,
    )


def norm_apply(values, gain_vector):
    row_mean = jnp.mean(values, -1, keepdims=True)
    centred = values - row_mean
    row_var = jnp.mean(centred * centred, -1, keepdims=True)
    return centred * lax.rsqrt(row_var + NORM_EPS) * gain_vector


def gated_unit(hidden):
    width_ff = hidden.shape[1] // 2
    return jax.nn.gelu(hidden[:, :width_ff], approximate=False) * hidden[:, width_ff:]


def per_device(
    tokens,
    seq_lengths,
    norm1_gain,
    qkv_weight,
    out_weight,
    norm2_gain,
    in_weight,
    down_weight,
    cotangent,
):
    attn_parts = (
        lax.all_gather(norm1_gain, "fsdp", axis=0, tiled=True),
        lax.all_gather(qkv_weight, "fsdp", axis=0, tiled=True),
        lax.all_gather(out_weight, "fsdp", axis=0, tiled=True),
    )
    mlp_parts = (
        lax.all_gather(norm2_gain, "fsdp", axis=0, tiled=True),
        lax.all_gather(in_weight, "fsdp", axis=0, tiled=True),
        lax.all_gather(down_weight, "fsdp", axis=1, tiled=True),
    )
    gain_one = attn_parts[0].astype(jnp.float32)
    w_qkv = attn_parts[1]
    w_out = attn_parts[2]
    gain_two = mlp_parts[0].astype(jnp.float32)
    w_in = mlp_parts[1]
    w_down = mlp_parts[2]
    slot_count, model_width = tokens.shape
    head_count = model_width // HEAD
    segment, positions = slot_layout(seq_lengths, slot_count)
    segment = segment[0]
    positions = positions[0]
    cosine_table, sine_table = rope_tables(positions, HEAD)
    allowed = (segment[:, None] == segment[None, :])[None]
    score_scale = HEAD ** (-0.5)
    inputs = tokens.astype(jnp.float32)
    normed, norm_one_pull = jax.vjp(norm_apply, inputs, gain_one)
    normed_b = normed.astype(jnp.bfloat16)
    joined_proj = jnp.dot(normed_b, w_qkv, preferred_element_type=jnp.float32)
    shape_heads = (slot_count, head_count, HEAD)

    def rope_pair(raw_queries, raw_keys):
        return (
            rotate(raw_queries, cosine_table, sine_table),
            rotate(raw_keys, cosine_table, sine_table),
        )

    rotated, rope_pull = jax.vjp(
        rope_pair,
        joined_proj[:, :model_width].reshape(shape_heads),
        joined_proj[:, model_width : 2 * model_width].reshape(shape_heads),
    )
    queries_b = rotated[0].astype(jnp.bfloat16)
    keys_b = rotated[1].astype(jnp.bfloat16)
    values_b = joined_proj[:, 2 * model_width :].reshape(shape_heads).astype(jnp.bfloat16)

    def masked_scores():
        raw_scores = (
            jnp.einsum("thd,shd->hts", queries_b, keys_b, preferred_element_type=jnp.float32)
            * score_scale
        )
        return jnp.where(allowed, raw_scores, MASK_FILL)

    scores = masked_scores()
    row_top = jnp.max(scores, -1, keepdims=True)
    exponent = jnp.exp(scores - row_top)
    row_total = jnp.sum(exponent, -1, keepdims=True)
    probs_b = (exponent / row_total).astype(jnp.bfloat16)
    context_b = jnp.einsum("hts,shd->thd", probs_b, values_b, preferred_element_type=jnp.float32)
    context_b = context_b.reshape(slot_count, model_width).astype(jnp.bfloat16)
    middle = inputs + jnp.dot(context_b, w_out, preferred_element_type=jnp.float32)
    normed_two, norm_two_pull = jax.vjp(norm_apply, middle, gain_two)
    normed_two_b = normed_two.astype(jnp.bfloat16)
    hidden = jnp.dot(normed_two_b, w_in, preferred_element_type=jnp.float32)
    activated, gate_pull = jax.vjp(gated_unit, hidden)
    mixed_b = activated.astype(jnp.bfloat16)
    output = (middle + jnp.dot(mixed_b, w_down, preferred_element_type=jnp.float32)).astype(
        jnp.bfloat16
    )
    attn_back = (
        lax.all_gather(qkv_weight, "fsdp", axis=0, tiled=True),
        lax.all_gather(out_weight, "fsdp", axis=0, tiled=True),
    )
    mlp_back = (
        lax.all_gather(in_weight, "fsdp", axis=0, tiled=True),
        lax.all_gather(down_weight, "fsdp", axis=1, tiled=True),
    )
    w_qkv = attn_back[0]
    w_out = attn_back[1]
    w_in = mlp_back[0]
    w_down = mlp_back[1]
    grad_out_b = cotangent.astype(jnp.bfloat16)
    grad_down = jnp.einsum("tf,td->fd", mixed_b, grad_out_b, preferred_element_type=jnp.float32)
    grad_mixed = jnp.einsum("td,fd->tf", grad_out_b, w_down, preferred_element_type=jnp.float32)
    grad_hidden_b = gate_pull(grad_mixed)[0].astype(jnp.bfloat16)
    grad_in = jnp.einsum(
        "tc,tf->cf", normed_two_b, grad_hidden_b, preferred_element_type=jnp.float32
    )
    grad_normed_two = jnp.einsum(
        "tf,cf->tc", grad_hidden_b, w_in, preferred_element_type=jnp.float32
    )
    grad_mid_norm, grad_gain_two = norm_two_pull(grad_normed_two)
    grad_middle = cotangent + grad_mid_norm
    grad_middle_b = grad_middle.astype(jnp.bfloat16)
    grad_w_out = jnp.einsum(
        "tc,td->cd", context_b, grad_middle_b, preferred_element_type=jnp.float32
    )
    grad_context = jnp.einsum("td,cd->tc", grad_middle_b, w_out, preferred_element_type=jnp.float32)
    grad_context_b = grad_context.reshape(shape_heads).astype(jnp.bfloat16)
    probs_again = jnp.exp(masked_scores() - row_top) / row_total
    probs_again_b = probs_again.astype(jnp.bfloat16)
    grad_probs = jnp.einsum(
        "thd,shd->hts", grad_context_b, values_b, preferred_element_type=jnp.float32
    )
    grad_values = jnp.einsum(
        "hts,thd->shd", probs_again_b, grad_context_b, preferred_element_type=jnp.float32
    )
    row_inner = jnp.sum(probs_again * grad_probs, -1, keepdims=True)
    grad_scores_b = (probs_again * (grad_probs - row_inner)).astype(jnp.bfloat16)
    grad_queries = (
        jnp.einsum("hts,shd->thd", grad_scores_b, keys_b, preferred_element_type=jnp.float32)
        * score_scale
    )
    grad_keys = (
        jnp.einsum("hts,thd->shd", grad_scores_b, queries_b, preferred_element_type=jnp.float32)
        * score_scale
    )
    raw_grads = rope_pull((grad_queries, grad_keys))
    grad_joined_b = jnp.concatenate(
        [
            raw_grads[0].reshape(slot_count, model_width),
            raw_grads[1].reshape(slot_count, model_width),
            grad_values.reshape(slot_count, model_width),
        ],
        1,
    ).astype(jnp.bfloat16)
    grad_qkv = jnp.einsum("tc,tf->cf", normed_b, grad_joined_b, preferred_element_type=jnp.float32)
    grad_normed = jnp.einsum("tf,cf->tc", grad_joined_b, w_qkv, preferred_element_type=jnp.float32)
    grad_in_norm, grad_gain_one = norm_one_pull(grad_normed)
    grad_tokens = grad_middle + grad_in_norm
    mlp_shards = (
        lax.psum_scatter(
            grad_gain_two.astype(jnp.bfloat16), "fsdp", scatter_dimension=0, tiled=True
        ).astype(jnp.float32),
        lax.psum_scatter(
            grad_in.astype(jnp.bfloat16), "fsdp", scatter_dimension=0, tiled=True
        ).astype(jnp.float32),
        lax.psum_scatter(
            grad_down.astype(jnp.bfloat16), "fsdp", scatter_dimension=1, tiled=True
        ).astype(jnp.float32),
    )
    attn_shards = (
        lax.psum_scatter(
            grad_gain_one.astype(jnp.bfloat16), "fsdp", scatter_dimension=0, tiled=True
        ).astype(jnp.float32),
        lax.psum_scatter(
            grad_qkv.astype(jnp.bfloat16), "fsdp", scatter_dimension=0, tiled=True
        ).astype(jnp.float32),
        lax.psum_scatter(
            grad_w_out.astype(jnp.bfloat16), "fsdp", scatter_dimension=0, tiled=True
        ).astype(jnp.float32),
    )
    summed = (
        lax.psum(attn_shards[0].astype(jnp.bfloat16), "replica").astype(jnp.float32),
        lax.psum(attn_shards[1].astype(jnp.bfloat16), "replica").astype(jnp.float32),
        lax.psum(attn_shards[2].astype(jnp.bfloat16), "replica").astype(jnp.float32),
        lax.psum(mlp_shards[0].astype(jnp.bfloat16), "replica").astype(jnp.float32),
        lax.psum(mlp_shards[1].astype(jnp.bfloat16), "replica").astype(jnp.float32),
        lax.psum(mlp_shards[2].astype(jnp.bfloat16), "replica").astype(jnp.float32),
    )
    return (output, grad_tokens, summed[0], summed[1], summed[2], summed[3], summed[4], summed[5])


def solution(mesh):
    return jax.shard_map(
        per_device,
        mesh=mesh,
        in_specs=(
            P(("replica", "fsdp"), None),
            P(("replica", "fsdp"), None),
            P("fsdp"),
            P("fsdp", None),
            P("fsdp", None),
            P("fsdp"),
            P("fsdp", None),
            P(None, "fsdp"),
            P(("replica", "fsdp"), None),
        ),
        out_specs=(
            P(("replica", "fsdp"), None),
            P(("replica", "fsdp"), None),
            P("fsdp"),
            P("fsdp", None),
            P("fsdp", None),
            P("fsdp"),
            P("fsdp", None),
            P(None, "fsdp"),
        ),
        check_vma=False,
    )
```

profile of v0, /device:TPU:0, one launch (start us, length us, event | category | flops | bytes accessed | tf_op | source)
XLA Modules:
  0.0 408.3 jit_solution(549852657426103821)
XLA Ops:
  16.4 15.3 %all-reduce.11 = (bf16[768]{0:T(1024)(128)(2,1)S(1)}, bf16[768]{0:T(1024)(128)(2,1)S(1)}) all-reduce(bf16[768]{0:T(1024)(128)(2,1)S(1)} %dynamic-update-slice, bf16[768]{0:T(1024)(128)(2,1)S(1)} %dynamic-update-slice.1), channel_id=1, replica_groups=mesh['replica'=4,'fsdp'=8] {'fsdp'}, use_global_device_ids=true, to_apply=%add.6 | all-reduce | flops 1536 | bytes 6144
  31.7 15.0 %all-gather.5.cloned.1.call-done = bf16[768,2304]{1,0:T(8,128)(2,1)} async-done(((bf16[96,2304]{1,0:T(8,128)(2,1)}), bf16[768,2304]{1,0:T(8,128)(2,1)}) %all-gather.5.cloned.1.call-update) | async-done | bytes 3538960 | tf_op jit(solution)/shard_map/all_gather | solution.py:72
  46.7 3.1 fusion.55
  52.2 2.9 fusion.64
  55.1 2.4 convolution_convert_fusion.6
  57.5 15.2 %all-gather.7.cloned.1.call-done = bf16[768,768]{1,0:T(8,128)(2,1)} async-done(((bf16[96,768]{1,0:T(8,128)(2,1)}), bf16[768,768]{1,0:T(8,128)(2,1)}) %all-gather.7.cloned.1.call-update) | async-done | bytes 1179664 | tf_op jit(solution)/shard_map/all_gather | solution.py:73
  75.9 32.7 %all-gather.9.cloned.1.call-done = bf16[768,2304]{1,0:T(8,128)(2,1)} async-done(((bf16[96,2304]{1,0:T(8,128)(2,1)}), bf16[768,2304]{1,0:T(8,128)(2,1)}) %all-gather.9.cloned.1.call-update) | async-done | bytes 3538960 | tf_op jit(solution)/shard_map/all_gather | solution.py:77
  108.6 3.2 fusion.58
  111.7 25.2 %all-gather.11.cloned.1.call-done = bf16[1152,768]{0,1:T(8,128)(2,1)} async-done(((bf16[1152,96]{0,1:T(8,128)(2,1)}), bf16[1152,768]{0,1:T(8,128)(2,1)}) %all-gather.11.cloned.1.call-update) | async-done | bytes 1769488 | tf_op jit(solution)/shard_map/all_gather | solution.py:78
  136.9 4.6 %fusion.28 = (f32[256,1152]{1,0:T(8,128)S(1)}, f32[256,1152]{1,0:T(8,128)S(1)}, f32[256,1152]{1,0:T(8,128)S(1)}) fusion(f32[256,2304]{1,0:T(8,128)S(1)} %fusion.58, bf16[1152,768]{0,1:T(8,128)(2,1)} %all-gather.11.cloned.1.call-done, f32[256,768]{1,0:T(8,128)} %param.17), kind=kOutput, calls=%fused_computation.81 | convolution fusion | flops 472350720 | bytes 7274496 | tf_op jit(solution)/shard_map/td,fd->tf/dot_general | solution.py:152
  150.5 2.0 convolution_convert_fusion.2
  153.1 4.7 %convolution_convert_fusion = bf16[768,2304]{1,0:T(8,128)(2,1)} fusion(f32[256,1152]{1,0:T(8,128)} %copy-done.2, f32[256,1152]{1,0:T(8,128)} %copy-done.9, f32[256,768]{1,0:T(8,128)S(1)} %get-tuple-element.51, f32[768]{0:T(1024)S(1)} %convert_element_type.123, f32[256]{0:T(256)S(1)} %copy-done.31, f32[256]{0:T(256)S(1)} %broadcast_multiply_fusion), kind=kOutput, calls=%fused_computation.1 | convolution fusion | flops 909705216 | bytes 6689792 | tf_op jit(solution)/shard_map/tc,tf->cf/dot_general | solution.py:154
  157.9 1.9 convolution_convert_fusion.5
  160.7 2.8 multiply_reduce_fusion
  168.7 3.2 convolution_convert_fusion.1
  172.6 13.9 %reduce-scatter.7.cloned.1.call-done = bf16[96,768]{1,0:T(8,128)(2,1)} async-done(((bf16[768,768]{1,0:T(8,128)(2,1)}), bf16[96,768]{1,0:T(8,128)(2,1)}) %reduce-scatter.7.cloned.1.call-update) | async-done | bytes 147472 | tf_op jit(solution)/shard_map/reduce_scatter | solution.py:217
  186.4 43.0 %reduce-scatter.11.cloned.1.call-done = bf16[1152,96]{0,1:T(8,128)(2,1)} async-done(((bf16[1152,768]{0,1:T(8,128)(2,1)}), bf16[1152,96]{0,1:T(8,128)(2,1)}) %reduce-scatter.11.cloned.1.call-update) | async-done | bytes 221200 | tf_op jit(solution)/shard_map/reduce_scatter | solution.py:206
  229.4 52.0 %reduce-scatter.9.cloned.1.call-done = bf16[96,2304]{1,0:T(8,128)(2,1)} async-done(((bf16[768,2304]{1,0:T(8,128)(2,1)}), bf16[96,2304]{1,0:T(8,128)(2,1)}) %reduce-scatter.9.cloned.1.call-update) | async-done | bytes 442384 | tf_op jit(solution)/shard_map/reduce_scatter | solution.py:203
  281.4 52.0 %reduce-scatter.5.cloned.1.call-done = bf16[96,2304]{1,0:T(8,128)(2,1)} async-done(((bf16[768,2304]{1,0:T(8,128)(2,1)}), bf16[96,2304]{1,0:T(8,128)(2,1)}) %reduce-scatter.5.cloned.1.call-update) | async-done | bytes 442384 | tf_op jit(solution)/shard_map/reduce_scatter | solution.py:214
  333.5 3.6 fusion.24
  337.5 13.1 %all-reduce.10 = (bf16[768]{0:T(1024)(128)(2,1)S(1)}, bf16[768]{0:T(1024)(128)(2,1)S(1)}) all-reduce(bf16[768]{0:T(1024)(128)(2,1)S(1)} %get-tuple-element.10, bf16[768]{0:T(1024)(128)(2,1)S(1)} %get-tuple-element.8), channel_id=2, replica_groups=mesh['replica'=4,'fsdp'=8] {'fsdp'}, use_global_device_ids=true, to_apply=%region_12.13.clone | all-reduce | flops 1536 | bytes 6144
  350.8 12.4 %all-reduce.12 = (bf16[96]{0:T(256)(128)(2,1)S(1)}, bf16[96]{0:T(256)(128)(2,1)S(1)}) all-reduce(bf16[96]{0:T(256)(128)(2,1)S(1)} %dynamic-slice.3, bf16[96]{0:T(256)(128)(2,1)S(1)} %dynamic-slice.5), channel_id=1, replica_groups=mesh['replica'=4,'fsdp'=8] {'replica'}, use_global_device_ids=true, to_apply=%region_13.14 | all-reduce | flops 192 | bytes 768 | tf_op jit(solution)/shard_map/psum | solution.py:222
  367.4 28.9 %all-reduce.16.cloned.1.call-done = (bf16[96,2304]{1,0:T(8,128)(2,1)}, bf16[96,768]{1,0:T(8,128)(2,1)}, bf16[96,2304]{1,0:T(8,128)(2,1)}, bf16[1152,96]{0,1:T(8,128)(2,1)}) async-done(((bf16[96,2304]{1,0:T(8,128)(2,1)}, bf16[96,768]{1,0:T(8,128)(2,1)}, bf16[96,2304]{1,0:T(8,128)(2,1)}, bf16[1152,96]{0,1:T(8,128)(2,1)}), (bf16[96,2304]{1,0:T(8,128)(2,1)}, bf16[96,768]{1,0:T(8,128)(2,1)}, ...) | async-done | bytes 1253392 | tf_op jit(solution)/shard_map/psum | solution.py:223
  398.0 2.0 convert_element_type.136
  (161 shorter events, 36.5 us)
Async XLA Ops:
  7.2 7.4 %copy-start.40 = (u32[32]{0:T(128)S(1)}, u32[32]{0:T(128)}, u32[]{:S(2)}) copy-start(u32[32]{0:T(128)} %constant.113) | copy-start | bytes 388
  7.2 8.7 %copy-start.42 = (bf16[96]{0:T(256)(128)(2,1)S(1)}, bf16[96]{0:T(256)(128)(2,1)}, u32[]{:S(2)}) copy-start(bf16[96]{0:T(256)(128)(2,1)} %param.11) | copy-start | bytes 580
  7.2 8.9 %copy-start.43 = (bf16[96]{0:T(256)(128)(2,1)S(1)}, bf16[96]{0:T(256)(128)(2,1)}, u32[]{:S(2)}) copy-start(bf16[96]{0:T(256)(128)(2,1)} %param.14) | copy-start | bytes 580
  7.2 39.5 %all-gather.5.cloned.1.call-start = ((), (), s32[]{:S(2)}) async-start(), calls=%async_computation.4 | async-start | bytes 3981312 | tf_op jit(solution)/shard_map/all_gather | solution.py:72
  8.0 64.8 %all-gather.7.cloned.1.call-start = ((), (), s32[]{:S(2)}) async-start(), calls=%async_computation.5 | async-start | bytes 1327104 | tf_op jit(solution)/shard_map/all_gather | solution.py:73
  8.7 99.9 %all-gather.9.cloned.1.call-start = ((), (), s32[]{:S(2)}) async-start(), calls=%async_computation.6 | async-start | bytes 3981312 | tf_op jit(solution)/shard_map/all_gather | solution.py:77
  9.4 127.5 %all-gather.11.cloned.1.call-start = ((), (), s32[]{:S(2)}) async-start(), calls=%async_computation.7 | async-start | bytes 1990656 | tf_op jit(solution)/shard_map/all_gather | solution.py:78
  10.0 176.4 %reduce-scatter.7.cloned.1.call-start = ((), (), s32[]{:S(2)}) async-start(), calls=%async_computation.9 | async-start | bytes 1327104 | tf_op jit(solution)/shard_map/reduce_scatter | solution.py:217
  10.5 39.4 %copy-start.36 = (f32[256]{0:T(256)}, f32[256]{0:T(256)S(1)}, u32[]{:S(2)}) copy-start(f32[256]{0:T(256)S(1)} %fusion.23) | copy-start | bytes 3076
  14.6 35.3 %copy-start.34 = (f32[256]{0:T(256)}, f32[256]{0:T(256)S(1)}, u32[]{:S(2)}) copy-start(f32[256]{0:T(256)S(1)} %fusion.40) | copy-start | bytes 3076
  50.5 4.6 %copy-start.19 = (bf16[256,768]{0,1:T(8,128)(2,1)}, bf16[256,768]{0,1:T(8,128)(2,1)S(1)}, u32[]{:S(2)}) copy-start(bf16[256,768]{0,1:T(8,128)(2,1)S(1)} %copy.37) | copy-start | bytes 1179652
  51.6 3.5 copy-start.10
  51.6 3.5 copy-start.12
  51.6 3.5 copy-start.14
  51.6 3.5 copy-start.16
  57.5 17.1 %copy-start.7 = (bf16[12,64,256]{2,1,0:T(8,128)(2,1)}, bf16[12,64,256]{2,1,0:T(8,128)(2,1)S(1)}, u32[]{:S(2)}) copy-start(bf16[12,64,256]{2,1,0:T(8,128)(2,1)S(1)} %convolution_convert_fusion.6) | copy-start | bytes 1179652
  149.5 79.9 %reduce-scatter.11.cloned.1.call-start = ((), (), s32[]{:S(2)}) async-start(), calls=%async_computation.11 | async-start | bytes 1990656 | tf_op jit(solution)/shard_map/reduce_scatter | solution.py:206
  152.5 128.9 %reduce-scatter.9.cloned.1.call-start = ((), (), s32[]{:S(2)}) async-start(), calls=%async_computation.10 | async-start | bytes 3981312 | tf_op jit(solution)/shard_map/reduce_scatter | solution.py:203
  157.8 175.6 %reduce-scatter.5.cloned.1.call-start = ((), (), s32[]{:S(2)}) async-start(), calls=%async_computation.8 | async-start | bytes 3981312 | tf_op jit(solution)/shard_map/reduce_scatter | solution.py:214
  168.5 3.3 copy-start.44
  171.9 224.5 %all-reduce.16.cloned.1.call-start = ((), (), s32[]{:S(2)}) async-start(), calls=%async_computation.12 | async-start | bytes 2506752 | tf_op jit(solution)/shard_map/psum | solution.py:223
  333.4 3.6 copy-start.37
  396.3 3.7 copy-start.28
  396.3 4.5 %copy-start.18 = (bf16[96,2304]{1,0:T(8,128)(2,1)S(1)}, bf16[96,2304]{1,0:T(8,128)(2,1)}, u32[]{:S(2)}) copy-start(bf16[96,2304]{1,0:T(8,128)(2,1)} %get-tuple-element.20) | copy-start | bytes 1327108
  (30 other events, 47.3 us)
Sparse Core Ops, SparseCore 0:
  9.9 36.7 all-gather.4
  48.6 24.0 all-gather.6
  74.6 33.9 all-gather.8
  110.3 26.5 all-gather.10
  149.6 36.7 reduce-scatter.6
  190.0 39.3 reduce-scatter.10
  233.3 48.0 reduce-scatter.8
  285.3 48.0 reduce-scatter.4
  336.3 59.9 all-reduce.15
where the time goes:
time: 409 us; the launch traced here: 408 us
  waiting for transfers between devices  280 us (68%)
  matrix products  41.9 us (10%)
  blocking collectives  40.8 us (10%)
  between operations  17 us (4%)
  other arithmetic  14.6 us (4%)
  local copies, waits for them, and re-layouts  13 us (3%)
    reduce_scatter x1, waiting for transfers between devices, per_device(): lax.psum_scatter(grad_in.astype(jnp.bfloat16), 'fsdp', scatter_dimension=...  52 us
    reduce_scatter x1, waiting for transfers between devices, per_device(): lax.psum_scatter(grad_qkv.astype(jnp.bfloat16), 'fsdp', scatter_dimension...  52 us
    reduce_scatter x1, waiting for transfers between devices, per_device(): lax.psum_scatter(grad_down.astype(jnp.bfloat16), 'fsdp', scatter_dimensio...  43 us
    all_gather x1, waiting for transfers between devices, per_device(): lax.all_gather(in_weight, 'fsdp', axis=0, tiled=True)  32.7 us
    psum x1, waiting for transfers between devices, per_device(): lax.psum(attn_shards[1].astype(jnp.bfloat16), 'replica').astype(jnp.float32)  28.9 us
    unnamed x2, blocking collectives  28.4 us
    all_gather x1, waiting for transfers between devices, per_device(): lax.all_gather(down_weight, 'fsdp', axis=1, tiled=True)  25.2 us
    all_gather x1, waiting for transfers between devices, per_device(): lax.all_gather(out_weight, 'fsdp', axis=0, tiled=True)  15.2 us
  transfers between devices with their start and end apart: 9, of which 9 were waited for; matrix products, arithmetic and copies ran while one was open for 11% of the time, Pallas kernels for 0%

commit v1 on v0

--- a/solution.py
+++ b/solution.py
@@ -1,6 +1,8 @@
 import jax
 import jax.numpy as jnp
 from jax import lax
+from jax.experimental import pallas as pl
+from jax.experimental.pallas import tpu as pltpu
 from jax.sharding import PartitionSpec as P
 
 HEAD = 64
@@ -56,6 +58,175 @@
     return jax.nn.gelu(hidden[:, :width_ff], approximate=False) * hidden[:, width_ff:]
 
 
+CORE, ALONG_X, ALONG_Y = 1, 2, 4
+F32, BF16 = jnp.float32, jnp.bfloat16
+
+
+def swap(values, mask):
+    return lax.ppermute(values, "fsdp", [(i, i ^ mask) for i in range(8)])
+
+
+def gather_pieces(own):
+    half = own.shape[0] // 2
+    from_x = swap(own, ALONG_X)
+    from_y = swap(own, ALONG_Y)
+    diag_a = swap(from_y[:half], ALONG_X)
+    diag_b = swap(from_x[half:], ALONG_Y)
+    mine = [own, from_x, from_y, diag_a, diag_b]
+    return mine + [swap(piece, CORE) for piece in mine]
+
+
+PIECE_PLACES = [
+    (mask | core, first)
+    for core in (0, CORE)
+    for mask, first in ((0, 0), (ALONG_X, 0), (ALONG_Y, 0), (6, 0), (6, 1))
+]
+
+
+def assemble(pieces, widths):
+    own_rows = pieces[0].shape[0]
+    row_count = 8 * own_rows
+
+    def kernel(*refs):
+        sources, targets, semaphores = refs[:10], refs[10:-1], refs[-1]
+        me = lax.axis_index("fsdp")
+        copies = []
+        for at, (mask, first) in enumerate(PIECE_PLACES):
+            rows = pieces[at].shape[0]
+            start = pl.multiple_of((me ^ mask) * own_rows + first * (own_rows // 2), own_rows // 2)
+            lane = 0
+            for to, width in enumerate(widths):
+                copies.append(
+                    pltpu.make_async_copy(
+                        sources[at].at[:, pl.ds(lane, width)],
+                        targets[to].at[pl.ds(start, rows), :],
+                        semaphores.at[at, to],
+                    )
+                )
+                lane += width
+        for copy in copies:
+            copy.start()
+        for copy in copies:
+            copy.wait()
+
+    return pl.pallas_call(
+        kernel,
+        out_shape=[jax.ShapeDtypeStruct((row_count, width), BF16) for width in widths],
+        in_specs=[pl.BlockSpec(memory_space=pl.ANY)] * 10,
+        out_specs=[pl.BlockSpec(memory_space=pl.ANY)] * len(widths),
+        scratch_shapes=[pltpu.SemaphoreType.DMA((10, len(widths)))],
+        name="assemble",
+    )(*pieces)
+
+
+LEAVING = [(6, 0), (ALONG_X, 0), (6, 1), (ALONG_Y, 1), (ALONG_X, 1), (ALONG_Y, 0), (0, 0), (0, 1)]
+
+
+def weight_grad(rows_side, columns_side):
+    slots, model_width = rows_side.shape
+    width = columns_side.shape[1]
+    half = model_width // 16
+    step = 384
+
+    def kernel(rows_ref, columns_ref, keep_ref, send_ref, turned, picked):
+        me = lax.axis_index("fsdp")
+        turned[...] = rows_ref[...].astype(F32).T.astype(BF16)
+        for core in (0, CORE):
+            for at, (mask, first) in enumerate(LEAVING):
+                start = pl.multiple_of((me ^ (mask | core)) * (2 * half) + first * half, half)
+                picked[pl.ds((core * 8 + at) * half, half), :] = turned[pl.ds(start, half), :]
+        for lane in range(0, width, step):
+            product = jnp.dot(
+                picked[...], columns_ref[:, lane : lane + step], preferred_element_type=F32
+            ).astype(BF16)
+            keep_ref[:, lane : lane + step] = product[: 8 * half]
+            send_ref[:, lane : lane + step] = product[8 * half :]
+
+    vmem = pl.BlockSpec(memory_space=pltpu.VMEM)
+    shape = jax.ShapeDtypeStruct((8 * half, width), BF16)
+    return pl.pallas_call(
+        kernel,
+        out_shape=[shape, shape],
+        in_specs=[vmem, vmem],
+        out_specs=[vmem, vmem],
+        scratch_shapes=[
+            pltpu.VMEM((model_width, slots), BF16),
+            pltpu.VMEM((model_width, slots), BF16),
+        ],
+        compiler_params=pltpu.CompilerParams(vmem_limit_bytes=40 * 2**20),
+        cost_estimate=pl.CostEstimate(
+            flops=2 * slots * model_width * width,
+            bytes_accessed=2 * (slots * (model_width + width) + model_width * width),
+            transcendentals=0,
+        ),
+        name="weight_grad",
+    )(rows_side, columns_side)
+
+
+def gather_rows(own, widths):
+    if lax.axis_size("fsdp") == 8:
+        return assemble(gather_pieces(own), widths)
+    whole = lax.all_gather(own, "fsdp", axis=0, tiled=True)
+    edges = [sum(widths[:at]) for at in range(1, len(widths))]
+    return jnp.split(whole, edges, 1)
+
+
+def shard_grad(rows_side, columns_side):
+    if lax.axis_size("fsdp") == 8:
+        return scatter_sum(*weight_grad(rows_side, columns_side))
+    whole = jnp.einsum("tc,tf->cf", rows_side, columns_side, preferred_element_type=F32)
+    shard = lax.psum_scatter(whole.astype(BF16), "fsdp", scatter_dimension=0, tiled=True)
+    return shard.astype(F32)
+
+
+def add(*parts):
+    return sum(part.astype(F32) for part in parts).astype(BF16)
+
+
+def scatter_sum(keep, send):
+    half = keep.shape[0] // 8
+    other = swap(send, CORE)
+
+    def chip(first, count):
+        rows = slice(first * half, (first + count) * half)
+        return add(keep[rows], other[rows])
+
+    by_x = swap(chip(0, 2), ALONG_X)
+    by_y = swap(chip(2, 2), ALONG_Y)
+    late_x = swap(add(keep[4 * half : 5 * half], other[4 * half : 5 * half], by_y[:half]), ALONG_X)
+    late_y = swap(add(keep[5 * half : 6 * half], other[5 * half : 6 * half], by_x[:half]), ALONG_Y)
+    own = keep[6 * half :].astype(F32) + other[6 * half :].astype(F32)
+    own += jnp.concatenate([by_x[half:], by_y[half:]], 0).astype(F32)
+    own += jnp.concatenate([late_y, late_x], 0).astype(F32)
+    return own
+
+
+def copies_sum(values):
+    copies = lax.axis_size("replica")
+    me = lax.axis_index("replica")
+    rows, width = values.shape
+    part = rows // copies
+    narrow = values.astype(BF16)
+
+    def shift(array, by):
+        return lax.ppermute(array, "replica", [(i, (i + by) % copies) for i in range(copies)])
+
+    def part_of(array, at):
+        return lax.dynamic_slice_in_dim(array, at * part, part, 0)
+
+    total = part_of(values, me)
+    for by in range(1, copies):
+        total += shift(part_of(narrow, (me + by) % copies), by).astype(F32)
+    total = total.astype(BF16)
+    result = jnp.zeros((copies, part, width), BF16)
+    result = lax.dynamic_update_index_in_dim(result, total, me, 0)
+    for by in range(1, copies):
+        result = lax.dynamic_update_index_in_dim(
+            result, shift(total, by), (me + copies - by) % copies, 0
+        )
+    return result.reshape(rows, width).astype(F32)
+
+
 def per_device(
     tokens,
     seq_lengths,
@@ -67,22 +238,20 @@
     down_weight,
     cotangent,
 ):
-    attn_parts = (
-        lax.all_gather(norm1_gain, "fsdp", axis=0, tiled=True),
-        lax.all_gather(qkv_weight, "fsdp", axis=0, tiled=True),
-        lax.all_gather(out_weight, "fsdp", axis=0, tiled=True),
-    )
-    mlp_parts = (
-        lax.all_gather(norm2_gain, "fsdp", axis=0, tiled=True),
-        lax.all_gather(in_weight, "fsdp", axis=0, tiled=True),
-        lax.all_gather(down_weight, "fsdp", axis=1, tiled=True),
-    )
-    gain_one = attn_parts[0].astype(jnp.float32)
-    w_qkv = attn_parts[1]
-    w_out = attn_parts[2]
-    gain_two = mlp_parts[0].astype(jnp.float32)
-    w_in = mlp_parts[1]
-    w_down = mlp_parts[2]
+    wide = qkv_weight.shape[1]
+    out_width = out_weight.shape[1]
+    ff_width = down_weight.shape[0]
+    gain_columns = jnp.pad(
+        jnp.stack([norm1_gain, norm2_gain], 1), ((0, 0), (0, 126))
+    )
+    w_qkv, w_out, gains = gather_rows(
+        jnp.concatenate([qkv_weight, out_weight, gain_columns], 1), (wide, out_width, 128)
+    )
+    w_in, w_down_t = gather_rows(
+        jnp.concatenate([in_weight, down_weight.T], 1), (wide, ff_width)
+    )
+    gain_one = gains[:, 0].astype(F32)
+    gain_two = gains[:, 1].astype(F32)
     slot_count, model_width = tokens.shape
     head_count = model_width // HEAD
     segment, positions = slot_layout(seq_lengths, slot_count)
@@ -132,37 +301,21 @@
     hidden = jnp.dot(normed_two_b, w_in, preferred_element_type=jnp.float32)
     activated, gate_pull = jax.vjp(gated_unit, hidden)
     mixed_b = activated.astype(jnp.bfloat16)
-    output = (middle + jnp.dot(mixed_b, w_down, preferred_element_type=jnp.float32)).astype(
+    output = (middle + jnp.einsum("tf,df->td", mixed_b, w_down_t, preferred_element_type=jnp.float32)).astype(
         jnp.bfloat16
     )
-    attn_back = (
-        lax.all_gather(qkv_weight, "fsdp", axis=0, tiled=True),
-        lax.all_gather(out_weight, "fsdp", axis=0, tiled=True),
-    )
-    mlp_back = (
-        lax.all_gather(in_weight, "fsdp", axis=0, tiled=True),
-        lax.all_gather(down_weight, "fsdp", axis=1, tiled=True),
-    )
-    w_qkv = attn_back[0]
-    w_out = attn_back[1]
-    w_in = mlp_back[0]
-    w_down = mlp_back[1]
     grad_out_b = cotangent.astype(jnp.bfloat16)
-    grad_down = jnp.einsum("tf,td->fd", mixed_b, grad_out_b, preferred_element_type=jnp.float32)
-    grad_mixed = jnp.einsum("td,fd->tf", grad_out_b, w_down, preferred_element_type=jnp.float32)
+    down_shard = shard_grad(grad_out_b, mixed_b)
+    grad_mixed = jnp.einsum("td,df->tf", grad_out_b, w_down_t, preferred_element_type=jnp.float32)
     grad_hidden_b = gate_pull(grad_mixed)[0].astype(jnp.bfloat16)
-    grad_in = jnp.einsum(
-        "tc,tf->cf", normed_two_b, grad_hidden_b, preferred_element_type=jnp.float32
-    )
+    in_shard = shard_grad(normed_two_b, grad_hidden_b)
     grad_normed_two = jnp.einsum(
         "tf,cf->tc", grad_hidden_b, w_in, preferred_element_type=jnp.float32
     )
-    grad_mid_norm, grad_gain_two = norm_two_pull(grad_normed_two)
+    grad_mid_norm = norm_two_pull(grad_normed_two)[0]
     grad_middle = cotangent + grad_mid_norm
     grad_middle_b = grad_middle.astype(jnp.bfloat16)
-    grad_w_out = jnp.einsum(
-        "tc,td->cd", context_b, grad_middle_b, preferred_element_type=jnp.float32
-    )
+    out_shard = shard_grad(context_b, grad_middle_b)
     grad_context = jnp.einsum("td,cd->tc", grad_middle_b, w_out, preferred_element_type=jnp.float32)
     grad_context_b = grad_context.reshape(shape_heads).astype(jnp.bfloat16)
     probs_again = jnp.exp(masked_scores() - row_top) / row_total
@@ -192,41 +345,28 @@
         ],
         1,
     ).astype(jnp.bfloat16)
-    grad_qkv = jnp.einsum("tc,tf->cf", normed_b, grad_joined_b, preferred_element_type=jnp.float32)
+    qkv_shard = shard_grad(normed_b, grad_joined_b)
     grad_normed = jnp.einsum("tf,cf->tc", grad_joined_b, w_qkv, preferred_element_type=jnp.float32)
-    grad_in_norm, grad_gain_one = norm_one_pull(grad_normed)
+    grad_in_norm = norm_one_pull(grad_normed)[0]
     grad_tokens = grad_middle + grad_in_norm
-    mlp_shards = (
-        lax.psum_scatter(
-            grad_gain_two.astype(jnp.bfloat16), "fsdp", scatter_dimension=0, tiled=True
-        ).astype(jnp.float32),
-        lax.psum_scatter(
-            grad_in.astype(jnp.bfloat16), "fsdp", scatter_dimension=0, tiled=True
-        ).astype(jnp.float32),
-        lax.psum_scatter(
-            grad_down.astype(jnp.bfloat16), "fsdp", scatter_dimension=1, tiled=True
-        ).astype(jnp.float32),
-    )
-    attn_shards = (
-        lax.psum_scatter(
-            grad_gain_one.astype(jnp.bfloat16), "fsdp", scatter_dimension=0, tiled=True
-        ).astype(jnp.float32),
-        lax.psum_scatter(
-            grad_qkv.astype(jnp.bfloat16), "fsdp", scatter_dimension=0, tiled=True
-        ).astype(jnp.float32),
-        lax.psum_scatter(
-            grad_w_out.astype(jnp.bfloat16), "fsdp", scatter_dimension=0, tiled=True
-        ).astype(jnp.float32),
-    )
-    summed = (
-        lax.psum(attn_shards[0].astype(jnp.bfloat16), "replica").astype(jnp.float32),
-        lax.psum(attn_shards[1].astype(jnp.bfloat16), "replica").astype(jnp.float32),
-        lax.psum(attn_shards[2].astype(jnp.bfloat16), "replica").astype(jnp.float32),
-        lax.psum(mlp_shards[0].astype(jnp.bfloat16), "replica").astype(jnp.float32),
-        lax.psum(mlp_shards[1].astype(jnp.bfloat16), "replica").astype(jnp.float32),
-        lax.psum(mlp_shards[2].astype(jnp.bfloat16), "replica").astype(jnp.float32),
-    )
-    return (output, grad_tokens, summed[0], summed[1], summed[2], summed[3], summed[4], summed[5])
+    mlp_sum = copies_sum(jnp.concatenate([in_shard, down_shard], 1))
+    attn_sum = copies_sum(jnp.concatenate([qkv_shard, out_shard], 1))
+    grad_qkv, grad_w_out = attn_sum[:, :wide], attn_sum[:, wide:]
+    grad_in, grad_down = mlp_sum[:, :wide], mlp_sum[:, wide:].T
+
+    def gain_grad(weight, weight_sum, gain):
+        return jnp.sum(weight.astype(F32) * weight_sum, 1) / gain.astype(F32)
+
+    return (
+        output,
+        grad_tokens,
+        gain_grad(qkv_weight, grad_qkv, norm1_gain),
+        grad_qkv,
+        grad_w_out,
+        gain_grad(in_weight, grad_in, norm2_gain),
+        grad_in,
+        grad_down,
+    )
 
 
 def solution(mesh):

time: 409 us -> 528 us (1.29)
  Pallas kernels: 0 us -> 317 us
  waiting for transfers between devices: 280 us -> 74.2 us
  starting transfers between devices: 0.54 us -> 57.7 us
  blocking collectives: 40.8 us -> 0 us
  between operations: 17 us -> 3.04 us
  matrix products: 41.9 us -> 29.1 us
  local copies, waits for them, and re-layouts: 13 us -> 23.5 us
  other arithmetic: 14.6 us -> 22.7 us
    pallas_call x0 -> x6, Pallas kernels: none -> 317 us  [the longest x2 312 us: assemble(): pl.pallas_call(kernel, out_shape=[jax.ShapeDtypeStruct((row_count, width)...]
    reduce_scatter x4 -> x0, waiting for transfers between devices: 161 us -> none  [the longest x1 52 us: per_device(): lax.psum_scatter(grad_in.astype(jnp.bfloat16), 'fsdp', scatter_dimension=...]
    all_gather x4 -> x0, waiting for transfers between devices: 88.1 us -> none  [the longest x1 32.7 us: per_device(): lax.all_gather(in_weight, 'fsdp', axis=0, tiled=True)]
    ppermute x0 -> x50, waiting for transfers between devices: none -> 74.2 us  [the longest x38 57.6 us: swap(): return lax.ppermute(values, 'fsdp', [(i, i ^ mask) for i in range(8)])]
    ppermute x0 -> x50, starting transfers between devices: none -> 57.7 us  [the longest x38 30 us: swap(): return lax.ppermute(values, 'fsdp', [(i, i ^ mask) for i in range(8)])]
    psum x1 -> x0, waiting for transfers between devices: 28.9 us -> none  [per_device(): lax.psum(attn_shards[1].astype(jnp.bfloat16), 'replica').astype(jnp.float32)]
    unnamed x2 -> x0, blocking collectives: 28.4 us -> none
    dot_general x6 -> x2, matrix products: 17.4 us -> 4.89 us  [the longest x1 3.43 us: per_device(): jnp.einsum('td,df->tf', grad_out_b, w_down_t, preferred_element_type=jnp....]
  transfers between devices with their start and end apart: 9 -> 50, of which waited for: 9 -> 24; matrix products, arithmetic and copies ran while one was open for 11% -> 6% of each run, Pallas kernels for 0% -> 29%
where the time goes in v1:
time: 528 us; the launch traced here: 527 us
  Pallas kernels  317 us (60%)
  waiting for transfers between devices  74.2 us (14%)
  starting transfers between devices  57.7 us (11%)
  matrix products  29.1 us (6%)
  local copies, waits for them, and re-layouts  23.5 us (4%)
  other arithmetic  22.7 us (4%)
    pallas_call x2, Pallas kernels, assemble(): pl.pallas_call(kernel, out_shape=[jax.ShapeDtypeStruct((row_count, width)...  312 us
    ppermute x38, waiting for transfers between devices, swap(): return lax.ppermute(values, 'fsdp', [(i, i ^ mask) for i in range(8)])  57.6 us
    ppermute x38, starting transfers between devices, swap(): return lax.ppermute(values, 'fsdp', [(i, i ^ mask) for i in range(8)])  30 us
    ppermute x12, starting transfers between devices, shift(): lax.ppermute(array, 'replica', [(i, (i + by) % copies) for i in range(cop...  27.7 us
    ppermute x12, waiting for transfers between devices, shift(): lax.ppermute(array, 'replica', [(i, (i + by) % copies) for i in range(cop...  16.6 us
  transfers between devices with their start and end apart: 50, of which 24 were waited for; matrix products, arithmetic and copies ran while one was open for 6% of the time, Pallas kernels for 29%

profile of v1, /device:TPU:0, one launch (start us, length us, event | category | flops | bytes accessed | tf_op | source)
XLA Modules:
  0.0 527.3 jit_solution(14301749845781940956)
XLA Ops:
  2.7 3.0 collective-permute-start.1
  12.3 8.2 %collective-permute-done.1.refs_2_ = bf16[96,3200]{1,0:T(8,128)(2,1)S(1)} collective-permute-done((bf16[96,3200]{1,0:T(8,128)(2,1)S(1)}, bf16[96,3200]{1,0:T(8,128)(2,1)S(1)}, u32[]{:S(2)}, u32[]{:S(2)}) %collective-permute-start.1) | collective-permute-done | bytes 614432 | tf_op jit(solution)/shard_map/ppermute | solution.py:66
  24.2 10.6 %collective-permute-done.10.refs_2_ = bf16[96,3456]{1,0:T(8,128)(2,1)} collective-permute-done((bf16[96,3456]{1,0:T(8,128)(2,1)}, bf16[96,3456]{1,0:T(8,128)(2,1)}, u32[]{:S(2)}, u32[]{:S(2)}) %collective-permute-start.10) | collective-permute-done | bytes 663584 | tf_op jit(solution)/shard_map/ppermute | solution.py:66
  40.4 3.1 collective-permute-done.2.refs_3_
  43.5 5.5 %collective-permute-done.11.refs_3_ = bf16[48,3456]{1,0:T(8,128)(2,1)S(1)} collective-permute-done((bf16[48,3456]{1,0:T(8,128)(2,1)S(1)}, bf16[48,3456]{1,0:T(8,128)(2,1)S(1)}, u32[]{:S(2)}, u32[]{:S(2)}) %collective-permute-start.11) | collective-permute-done | bytes 331808 | tf_op jit(solution)/shard_map/ppermute | solution.py:66
  52.3 150.3 %assemble.2 = (bf16[768,2304]{1,0:T(8,128)(2,1)}, bf16[768,768]{1,0:T(8,128)(2,1)}, bf16[768,128]{1,0:T(8,128)(2,1)}) custom-call(bf16[96,3200]{1,0:T(8,128)(2,1)} %copy-done.18, bf16[96,3200]{1,0:T(8,128)(2,1)} %copy-done.28, bf16[96,3200]{1,0:T(8,128)(2,1)} %copy-done.27, bf16[48,3200]{1,0:T(8,128)(2,1)} %collective-permute-done.2.refs_3_, ...), custom_call_target="tpu_custom_call" | custom-call | tf_op jit(solution)/shard_map/assemble/pallas_call | solution.py:112
  204.1 3.1 fusion.65
  211.9 3.9 fusion.63
  219.8 162.1 %assemble.3 = (bf16[768,2304]{1,0:T(8,128)(2,1)}, bf16[768,1152]{1,0:T(8,128)(2,1)}) custom-call(bf16[96,3456]{1,0:T(8,128)(2,1)} %pad_maximum_fusion.3.refs_0_, bf16[96,3456]{1,0:T(8,128)(2,1)} %collective-permute-done.9.refs_1_, bf16[96,3456]{1,0:T(8,128)(2,1)} %collective-permute-done.10.refs_2_, bf16[48,3456]{1,0:T(8,128)(2,1)} %copy-done.42, ...), custom_call_target="tpu_custom_call" | custom-call | tf_op jit(solution)/shard_map/assemble/pallas_call | solution.py:112
  381.9 3.2 fusion.66
  385.1 3.4 fusion.29
  397.9 2.9 multiply_reduce_fusion
  416.6 3.3 fusion.25
  431.3 3.9 collective-permute-done.24
  453.7 8.7 %collective-permute-done.19 = bf16[96,2304]{1,0:T(8,128)(2,1)S(1)} collective-permute-done((bf16[96,2304]{1,0:T(8,128)(2,1)S(1)}, bf16[96,2304]{1,0:T(8,128)(2,1)S(1)}, u32[]{:S(2)}, u32[]{:S(2)}) %collective-permute-start.19) | collective-permute-done | bytes 442400 | tf_op jit(solution)/shard_map/ppermute | solution.py:66
  465.7 6.0 %collective-permute-done.35 = bf16[96,2304]{1,0:T(8,128)(2,1)S(1)} collective-permute-done((bf16[96,2304]{1,0:T(8,128)(2,1)S(1)}, bf16[96,2304]{1,0:T(8,128)(2,1)S(1)}, u32[]{:S(2)}, u32[]{:S(2)}) %collective-permute-start.35) | collective-permute-done | bytes 442400 | tf_op jit(solution)/shard_map/ppermute | solution.py:66
  477.1 2.6 collective-permute-start.29
  486.2 5.4 %collective-permute-done.29 = bf16[24,3072]{1,0:T(8,128)(2,1)S(1)} collective-permute-done((bf16[24,3072]{1,0:T(8,128)(2,1)S(1)}, bf16[24,3072]{1,0:T(8,128)(2,1)S(1)}, u32[]{:S(2)}, u32[]{:S(2)}) %collective-permute-start.29) | collective-permute-done | bytes 147488 | tf_op jit(solution)/shard_map/ppermute | solution.py:212
  491.8 6.5 %collective-permute-start.31 = (bf16[24,3072]{1,0:T(8,128)(2,1)S(1)}, bf16[24,3072]{1,0:T(8,128)(2,1)S(1)}, u32[]{:S(2)}, u32[]{:S(2)}) collective-permute-start(bf16[24,3072]{1,0:T(8,128)(2,1)S(1)} %get-tuple-element.43), channel_id=1, source_target_pairs={{0,8},{8,16},{16,24},{24,0},{1,9},{9,17},{17,25},{25,1},{2,10},{10... | collective-permute-start | bytes 442376 | tf_op jit(solution)/shard_map/ppermute | solution.py:212
  498.3 3.1 collective-permute-start.32
  501.4 5.8 %collective-permute-done.45 = bf16[24,3456]{1,0:T(8,128)(2,1)S(1)} collective-permute-done((bf16[24,3456]{1,0:T(8,128)(2,1)S(1)}, bf16[24,3456]{1,0:T(8,128)(2,1)S(1)}, u32[]{:S(2)}, u32[]{:S(2)}) %collective-permute-start.45) | collective-permute-done | bytes 165920 | tf_op jit(solution)/shard_map/ppermute | solution.py:212
  507.3 4.8 collective-permute-start.47
  512.1 3.2 collective-permute-start.48
  518.7 5.1 collective-permute-done.48
  (308 shorter events, 106.6 us)
Async XLA Ops:
  2.7 17.7 %collective-permute-start.1 = (bf16[96,3200]{1,0:T(8,128)(2,1)S(1)}, bf16[96,3200]{1,0:T(8,128)(2,1)S(1)}, u32[]{:S(2)}, u32[]{:S(2)}) collective-permute-start(bf16[96,3200]{1,0:T(8,128)(2,1)S(1)} %fusion.28.refs_0_), channel_id=1, source_target_pairs={{0,4},{1,5},{2,6},{3,7},{4,0},{5,1},{6,2},{7,3},{8,12},{9,13},{10,... | collective-permute-start | bytes 1843208 | tf_op jit(solution)/shard_map/ppermute | solution.py:66
  5.8 16.8 %collective-permute-start = (bf16[96,3200]{1,0:T(8,128)(2,1)S(1)}, bf16[96,3200]{1,0:T(8,128)(2,1)S(1)}, u32[]{:S(2)}, u32[]{:S(2)}) collective-permute-start(bf16[96,3200]{1,0:T(8,128)(2,1)S(1)} %fusion.28.refs_0_), channel_id=1, source_target_pairs={{0,2},{1,3},{2,0},{3,1},{4,6},{5,7},{6,4},{7,5},{8,10},{9,11},{10,... | collective-permute-start | bytes 1843208 | tf_op jit(solution)/shard_map/ppermute | solution.py:66
  7.3 28.5 %collective-permute-start.4 = (bf16[96,3200]{1,0:T(8,128)(2,1)S(1)}, bf16[96,3200]{1,0:T(8,128)(2,1)S(1)}, u32[]{:S(2)}, u32[]{:S(2)}) collective-permute-start(bf16[96,3200]{1,0:T(8,128)(2,1)S(1)} %fusion.28.refs_0_), channel_id=1, source_target_pairs={{0,1},{1,0},{2,3},{3,2},{4,5},{5,4},{6,7},{7,6},{8,9},{9,8},{10,11... | collective-permute-start | bytes 1843208 | tf_op jit(solution)/shard_map/ppermute | solution.py:66
  8.2 26.6 %collective-permute-start.10 = (bf16[96,3456]{1,0:T(8,128)(2,1)}, bf16[96,3456]{1,0:T(8,128)(2,1)}, u32[]{:S(2)}, u32[]{:S(2)}) collective-permute-start(bf16[96,3456]{1,0:T(8,128)(2,1)} %pad_maximum_fusion.3.refs_0_), channel_id=1, source_target_pairs={{0,4},{1,5},{2,6},{3,7},{4,0},{5,1},{6,2},{7,3},{8,12},{9,13},{10,... | collective-permute-start | bytes 1990664 | tf_op jit(solution)/shard_map/ppermute | solution.py:66
  8.7 28.2 %collective-permute-start.9 = (bf16[96,3456]{1,0:T(8,128)(2,1)}, bf16[96,3456]{1,0:T(8,128)(2,1)}, u32[]{:S(2)}, u32[]{:S(2)}) collective-permute-start(bf16[96,3456]{1,0:T(8,128)(2,1)} %pad_maximum_fusion.3.refs_0_), channel_id=1, source_target_pairs={{0,2},{1,3},{2,0},{3,1},{4,6},{5,7},{6,4},{7,5},{8,10},{9,11},{10,... | collective-permute-start | bytes 1990664 | tf_op jit(solution)/shard_map/ppermute | solution.py:66
  20.5 23.0 %collective-permute-start.2 = (bf16[48,3200]{1,0:T(8,128)(2,1)S(1)}, bf16[48,3200]{1,0:T(8,128)(2,1)}, u32[]{:S(2)}, u32[]{:S(2)}) collective-permute-start(bf16[48,3200]{1,0:T(8,128)(2,1)S(1)} %slice.309), channel_id=1, source_target_pairs={{0,2},{1,3},{2,0},{3,1},{4,6},{5,7},{6,4},{7,5},{8,10},{9,11},{10,... | collective-permute-start | bytes 921608 | tf_op jit(solution)/shard_map/ppermute | solution.py:66
  22.6 20.8 %collective-permute-start.3 = (bf16[48,3200]{1,0:T(8,128)(2,1)S(1)}, bf16[48,3200]{1,0:T(8,128)(2,1)}, u32[]{:S(2)}, u32[]{:S(2)}) collective-permute-start(bf16[48,3200]{1,0:T(8,128)(2,1)S(1)} %slice.310), channel_id=1, source_target_pairs={{0,4},{1,5},{2,6},{3,7},{4,0},{5,1},{6,2},{7,3},{8,12},{9,13},{10,... | collective-permute-start | bytes 921608 | tf_op jit(solution)/shard_map/ppermute | solution.py:66
  34.8 17.0 %collective-permute-start.5 = (bf16[96,3200]{1,0:T(8,128)(2,1)S(1)}, bf16[96,3200]{1,0:T(8,128)(2,1)}, u32[]{:S(2)}, u32[]{:S(2)}) collective-permute-start(bf16[96,3200]{1,0:T(8,128)(2,1)S(1)} %collective-permute-done.refs_1_), channel_id=1, source_target_pairs={{0,1},{1,0},{2,3},{3,2},{4,5},{5,4},{6,7},{7,6},{8,9},{9,8},{10,11... | collective-permute-start | bytes 1843208 | tf_op jit(solution)/shard_map/ppermute | solution.py:66
  35.8 16.4 %collective-permute-start.6 = (bf16[96,3200]{1,0:T(8,128)(2,1)S(1)}, bf16[96,3200]{1,0:T(8,128)(2,1)}, u32[]{:S(2)}, u32[]{:S(2)}) collective-permute-start(bf16[96,3200]{1,0:T(8,128)(2,1)S(1)} %collective-permute-done.1.refs_2_), channel_id=1, source_target_pairs={{0,1},{1,0},{2,3},{3,2},{4,5},{5,4},{6,7},{7,6},{8,9},{9,8},{10,11... | collective-permute-start | bytes 1843208 | tf_op jit(solution)/shard_map/ppermute | solution.py:66
  50.9 168.8 %collective-permute-start.13 = (bf16[96,3456]{1,0:T(8,128)(2,1)}, bf16[96,3456]{1,0:T(8,128)(2,1)}, u32[]{:S(2)}, u32[]{:S(2)}) collective-permute-start(bf16[96,3456]{1,0:T(8,128)(2,1)} %pad_maximum_fusion.3.refs_0_), channel_id=1, source_target_pairs={{0,1},{1,0},{2,3},{3,2},{4,5},{5,4},{6,7},{7,6},{8,9},{9,8},{10,11... | collective-permute-start | bytes 1990664 | tf_op jit(solution)/shard_map/ppermute | solution.py:66
  51.1 168.6 %collective-permute-start.14 = (bf16[96,3456]{1,0:T(8,128)(2,1)}, bf16[96,3456]{1,0:T(8,128)(2,1)}, u32[]{:S(2)}, u32[]{:S(2)}) collective-permute-start(bf16[96,3456]{1,0:T(8,128)(2,1)} %collective-permute-done.9.refs_1_), channel_id=1, source_target_pairs={{0,1},{1,0},{2,3},{3,2},{4,5},{5,4},{6,7},{7,6},{8,9},{9,8},{10,11... | collective-permute-start | bytes 1990664 | tf_op jit(solution)/shard_map/ppermute | solution.py:66
  51.7 168.1 %collective-permute-start.15 = (bf16[96,3456]{1,0:T(8,128)(2,1)}, bf16[96,3456]{1,0:T(8,128)(2,1)}, u32[]{:S(2)}, u32[]{:S(2)}) collective-permute-start(bf16[96,3456]{1,0:T(8,128)(2,1)} %collective-permute-done.10.refs_2_), channel_id=1, source_target_pairs={{0,1},{1,0},{2,3},{3,2},{4,5},{5,4},{6,7},{7,6},{8,9},{9,8},{10,11... | collective-permute-start | bytes 1990664 | tf_op jit(solution)/shard_map/ppermute | solution.py:66
  51.8 167.9 %collective-permute-start.16 = (bf16[48,3456]{1,0:T(8,128)(2,1)}, bf16[48,3456]{1,0:T(8,128)(2,1)}, u32[]{:S(2)}, u32[]{:S(2)}) collective-permute-start(bf16[48,3456]{1,0:T(8,128)(2,1)} %copy-done.42), channel_id=1, source_target_pairs={{0,1},{1,0},{2,3},{3,2},{4,5},{5,4},{6,7},{7,6},{8,9},{9,8},{10,11... | collective-permute-start | bytes 995336 | tf_op jit(solution)/shard_map/ppermute | solution.py:66
  52.2 167.5 %collective-permute-start.17 = (bf16[48,3456]{1,0:T(8,128)(2,1)}, bf16[48,3456]{1,0:T(8,128)(2,1)}, u32[]{:S(2)}, u32[]{:S(2)}) collective-permute-start(bf16[48,3456]{1,0:T(8,128)(2,1)} %collective-permute-done.12.refs_4_), channel_id=1, source_target_pairs={{0,1},{1,0},{2,3},{3,2},{4,5},{5,4},{6,7},{7,6},{8,9},{9,8},{10,11... | collective-permute-start | bytes 995336 | tf_op jit(solution)/shard_map/ppermute | solution.py:66
  420.0 32.1 %collective-permute-start.34 = (bf16[384,2304]{1,0:T(8,128)(2,1)S(1)}, bf16[384,2304]{1,0:T(8,128)(2,1)S(1)}, u32[]{:S(2)}, u32[]{:S(2)}) collective-permute-start(bf16[384,2304]{1,0:T(8,128)(2,1)S(1)} %copy-done.3), channel_id=1, source_target_pairs={{0,1},{1,0},{2,3},{3,2},{4,5},{5,4},{6,7},{7,6},{8,9},{9,8},{10,11... | collective-permute-start | bytes 5308424 | tf_op jit(solution)/shard_map/ppermute | solution.py:66
  423.1 25.4 %collective-permute-start.18 = (bf16[384,2304]{1,0:T(8,128)(2,1)S(1)}, bf16[384,2304]{1,0:T(8,128)(2,1)S(1)}, u32[]{:S(2)}, u32[]{:S(2)}) collective-permute-start(bf16[384,2304]{1,0:T(8,128)(2,1)S(1)} %get-tuple-element.27), channel_id=1, source_target_pairs={{0,1},{1,0},{2,3},{3,2},{4,5},{5,4},{6,7},{7,6},{8,9},{9,8},{10,11... | collective-permute-start | bytes 5308424 | tf_op jit(solution)/shard_map/ppermute | solution.py:66
  452.3 19.4 %collective-permute-start.35 = (bf16[96,2304]{1,0:T(8,128)(2,1)S(1)}, bf16[96,2304]{1,0:T(8,128)(2,1)S(1)}, u32[]{:S(2)}, u32[]{:S(2)}) collective-permute-start(bf16[96,2304]{1,0:T(8,128)(2,1)S(1)} %get-tuple-element.50), channel_id=1, source_target_pairs={{0,2},{1,3},{2,0},{3,1},{4,6},{5,7},{6,4},{7,5},{8,10},{9,11},{10,... | collective-permute-start | bytes 1327112 | tf_op jit(solution)/shard_map/ppermute | solution.py:66
  452.6 20.1 %collective-permute-start.36 = (bf16[96,2304]{1,0:T(8,128)(2,1)S(1)}, bf16[96,2304]{1,0:T(8,128)(2,1)S(1)}, u32[]{:S(2)}, u32[]{:S(2)}) collective-permute-start(bf16[96,2304]{1,0:T(8,128)(2,1)S(1)} %get-tuple-element.51), channel_id=1, source_target_pairs={{0,4},{1,5},{2,6},{3,7},{4,0},{5,1},{6,2},{7,3},{8,12},{9,13},{10,... | collective-permute-start | bytes 1327112 | tf_op jit(solution)/shard_map/ppermute | solution.py:66
  477.1 14.6 %collective-permute-start.29 = (bf16[24,3072]{1,0:T(8,128)(2,1)S(1)}, bf16[24,3072]{1,0:T(8,128)(2,1)S(1)}, u32[]{:S(2)}, u32[]{:S(2)}) collective-permute-start(bf16[24,3072]{1,0:T(8,128)(2,1)S(1)} %get-tuple-element.81), channel_id=1, source_target_pairs={{0,16},{8,24},{16,0},{24,8},{1,17},{9,25},{17,1},{25,9},{2,18},{10... | collective-permute-start | bytes 442376 | tf_op jit(solution)/shard_map/ppermute | solution.py:212
  481.4 20.0 %collective-permute-start.44 = (bf16[24,3456]{1,0:T(8,128)(2,1)S(1)}, bf16[24,3456]{1,0:T(8,128)(2,1)S(1)}, u32[]{:S(2)}, u32[]{:S(2)}) collective-permute-start(bf16[24,3456]{1,0:T(8,128)(2,1)S(1)} %get-tuple-element.76), channel_id=1, source_target_pairs={{0,8},{8,16},{16,24},{24,0},{1,9},{9,17},{17,25},{25,1},{2,10},{10... | collective-permute-start | bytes 497672 | tf_op jit(solution)/shard_map/ppermute | solution.py:212
  482.1 25.0 %collective-permute-start.45 = (bf16[24,3456]{1,0:T(8,128)(2,1)S(1)}, bf16[24,3456]{1,0:T(8,128)(2,1)S(1)}, u32[]{:S(2)}, u32[]{:S(2)}) collective-permute-start(bf16[24,3456]{1,0:T(8,128)(2,1)S(1)} %get-tuple-element.78), channel_id=1, source_target_pairs={{0,16},{8,24},{16,0},{24,8},{1,17},{9,25},{17,1},{25,9},{2,18},{10... | collective-permute-start | bytes 497672 | tf_op jit(solution)/shard_map/ppermute | solution.py:212
  484.1 23.0 %collective-permute-start.46 = (bf16[24,3456]{1,0:T(8,128)(2,1)S(1)}, bf16[24,3456]{1,0:T(8,128)(2,1)S(1)}, u32[]{:S(2)}, u32[]{:S(2)}) collective-permute-start(bf16[24,3456]{1,0:T(8,128)(2,1)S(1)} %get-tuple-element.77), channel_id=1, source_target_pairs={{0,24},{8,0},{16,8},{24,16},{1,25},{9,1},{17,9},{25,17},{2,26},{10... | collective-permute-start | bytes 497672 | tf_op jit(solution)/shard_map/ppermute | solution.py:212
  491.8 23.5 %collective-permute-start.31 = (bf16[24,3072]{1,0:T(8,128)(2,1)S(1)}, bf16[24,3072]{1,0:T(8,128)(2,1)S(1)}, u32[]{:S(2)}, u32[]{:S(2)}) collective-permute-start(bf16[24,3072]{1,0:T(8,128)(2,1)S(1)} %get-tuple-element.43), channel_id=1, source_target_pairs={{0,8},{8,16},{16,24},{24,0},{1,9},{9,17},{17,25},{25,1},{2,10},{10... | collective-permute-start | bytes 442376 | tf_op jit(solution)/shard_map/ppermute | solution.py:212
  498.3 17.1 %collective-permute-start.32 = (bf16[24,3072]{1,0:T(8,128)(2,1)S(1)}, bf16[24,3072]{1,0:T(8,128)(2,1)S(1)}, u32[]{:S(2)}, u32[]{:S(2)}) collective-permute-start(bf16[24,3072]{1,0:T(8,128)(2,1)S(1)} %get-tuple-element.43), channel_id=1, source_target_pairs={{0,16},{8,24},{16,0},{24,8},{1,17},{9,25},{17,1},{25,9},{2,18},{10... | collective-permute-start | bytes 442376 | tf_op jit(solution)/shard_map/ppermute | solution.py:212
  (87 other events, 1290.5 us)

commit v2 on v1

v2 whole, which is shorter than its diff:
```python
import jax
import jax.numpy as jnp
from jax import lax
from jax.experimental import pallas as pl
from jax.experimental.pallas import tpu as pltpu
from jax.sharding import PartitionSpec as P

HEAD = 64


NORM_EPS = 1e-05
ROPE_BASE = 160000.0
MASK_FILL = -1000000000.0


def slot_layout(length_pairs, slot_count):
    slot_index = jnp.arange(slot_count, dtype=jnp.int32)[None, :]
    first_length = length_pairs[:, 0:1]
    both_lengths = first_length + length_pairs[:, 1:2]
    segment = jnp.where(
        slot_index < first_length, 0, jnp.where(slot_index < both_lengths, 1, 2)
    ).astype(jnp.int32)
    begin = jnp.where(segment == 0, 0, jnp.where(segment == 1, first_length, both_lengths))
    return (segment, slot_index - begin)


def rope_tables(positions, head_size):
    half_size = head_size // 2
    frequency = ROPE_BASE ** (-(jnp.arange(half_size, dtype=jnp.float32) * 2.0) / head_size)
    angles = positions.astype(jnp.float32)[:, None] * frequency[None, :]
    return (jnp.cos(angles), jnp.sin(angles))


CORE, ALONG_X, ALONG_Y = 1, 2, 4
F32, BF16 = jnp.float32, jnp.bfloat16
VMEM = pl.BlockSpec(memory_space=pltpu.VMEM)
LANES = 128
STEP = 384


def run_kernel(body, name, outs, scratch, operands, scalars=0, flops=0):
    smem = pl.BlockSpec(memory_space=pltpu.SMEM)
    return pl.pallas_call(
        body,
        out_shape=[jax.ShapeDtypeStruct(shape, kind) for shape, kind in outs],
        in_specs=[smem] * scalars + [VMEM] * (len(operands) - scalars),
        out_specs=[VMEM] * len(outs),
        scratch_shapes=scratch,
        compiler_params=pltpu.CompilerParams(vmem_limit_bytes=48 * 2**20),
        cost_estimate=pl.CostEstimate(flops=flops, bytes_accessed=0, transcendentals=0),
        name=name,
    )(*operands)


def swap(values, mask):
    return lax.ppermute(values, "fsdp", [(i, i ^ mask) for i in range(8)])


def gather_pieces(own):
    half = own.shape[0] // 2
    from_x = swap(own, ALONG_X)
    from_y = swap(own, ALONG_Y)
    diag_a = swap(from_y[:half], ALONG_X)
    diag_b = swap(from_x[half:], ALONG_Y)
    mine = [own, from_x, from_y, diag_a, diag_b]
    return mine + [swap(piece, CORE) for piece in mine]


PIECE_PLACES = [
    (mask | core, first)
    for core in (0, CORE)
    for mask, first in ((0, 0), (ALONG_X, 0), (ALONG_Y, 0), (6, 0), (6, 1))
]


def gathered(own):
    if lax.axis_size("fsdp") == 8:
        return gather_pieces(own)
    return [lax.all_gather(own, "fsdp", axis=0, tiled=True)]


def lay_out(pieces, targets):
    if len(pieces) == 1:
        places = [(0, 0)]
        me, own_rows = 0, pieces[0].shape[0]
    else:
        places = PIECE_PLACES
        me, own_rows = lax.axis_index("fsdp"), pieces[0].shape[0]
    for piece, (mask, first) in zip(pieces, places):
        rows = piece.shape[0]
        start = (me ^ mask) * own_rows + first * (own_rows // 2)
        start = 0 if len(pieces) == 1 else pl.multiple_of(start, own_rows // 2)
        lane = 0
        for target in targets:
            width = target.shape[1]
            target[pl.ds(start, rows), :] = piece[:, lane : lane + width]
            lane += width


LEAVING = [(6, 0), (ALONG_X, 0), (6, 1), (ALONG_Y, 1), (ALONG_X, 1), (ALONG_Y, 0), (0, 0), (0, 1)]


def pick_rows(values, turned, picked):
    if picked is None:
        turned[...] = values.astype(F32).T.astype(BF16)
        return
    half = turned.shape[0] // 16
    me = lax.axis_index("fsdp")
    turned[...] = values.astype(F32).T.astype(BF16)
    for core in (0, CORE):
        for at, (mask, first) in enumerate(LEAVING):
            start = pl.multiple_of((me ^ (mask | core)) * (2 * half) + first * half, half)
            picked[pl.ds((core * 8 + at) * half, half), :] = turned[pl.ds(start, half), :]


def write_grad(lhs, columns, outs):
    width = columns.shape[1]
    for lane in range(0, width, STEP):
        product = jnp.dot(
            lhs[...], columns[:, lane : lane + STEP], preferred_element_type=F32
        ).astype(BF16)
        row = 0
        for out in outs:
            out[:, lane : lane + STEP] = product[row : row + out.shape[0]]
            row += out.shape[0]


def grad_outs(model_width, width):
    if lax.axis_size("fsdp") == 8:
        return [((model_width // 2, width), BF16)] * 2
    return [((model_width, width), BF16)]


def grad_scratch(model_width, slots):
    one = pltpu.VMEM((model_width, slots), BF16)
    return [one, one] if lax.axis_size("fsdp") == 8 else [one]


def write_weight_grad(rows_side, columns, outs, scratch):
    pick_rows(rows_side, scratch[0], scratch[1] if len(scratch) > 1 else None)
    write_grad(scratch[-1], columns, outs)


def dot_nt(a, b):
    return lax.dot_general(a, b, (((1,), (1,)), ((), ())), preferred_element_type=F32)


def dot_tn(a, b):
    return lax.dot_general(a, b, (((0,), (0,)), ((), ())), preferred_element_type=F32)


def dot_nn(a, b):
    return jnp.dot(a, b, preferred_element_type=F32)


def normalised(values):
    mean = jnp.mean(values, -1, keepdims=True)
    centred = values - mean
    scale = lax.rsqrt(jnp.mean(centred * centred, -1, keepdims=True) + NORM_EPS)
    return centred * scale, scale


def norm_back(grad, xhat, scale, gain):
    scaled = grad * gain
    mean = jnp.mean(scaled, -1, keepdims=True)
    along = jnp.mean(scaled * xhat, -1, keepdims=True)
    return scale * (scaled - mean - xhat * along)


def turn_halves(block, cosine, sine):
    lane = lax.broadcasted_iota(jnp.int32, block.shape, 1)
    low_half = (lane % HEAD) < HEAD // 2
    other = jnp.where(
        low_half,
        pltpu.roll(block, LANES - HEAD // 2, 1),
        pltpu.roll(block, HEAD // 2, 1),
    )
    return block * cosine + other * sine


def head_lanes(shape, head):
    lane = lax.broadcasted_iota(jnp.int32, shape, 1)
    return (lane // HEAD) == head


def only(values, head):
    return jnp.where(head_lanes(values.shape, head), values, jnp.zeros_like(values))


def attention_forward(lengths, tokens, cosine, sine, pieces, qkv_width, out_width):
    slots, model_width = tokens.shape
    count = len(pieces)

    def body(*refs):
        lengths_ref, tokens_ref, cosine_ref, sine_ref = refs[:4]
        piece_refs = refs[4 : 4 + count]
        (h1_ref, q_ref, k_ref, v_ref, probs_ref, context_ref, middle_ref, h2_ref, w_qkv, w_out,
         gain_rows, gain_columns, joined) = refs[4 + count :]
        lay_out(piece_refs, [w_qkv, w_out, gain_columns])
        gain_rows[...] = gain_columns[...].astype(F32).T[:8]
        inputs = tokens_ref[...].astype(F32)
        h1_ref[...] = (normalised(inputs)[0] * gain_rows[0:1, :]).astype(BF16)
        for lane in range(0, qkv_width, model_width):
            joined[:, lane : lane + model_width] = dot_nn(
                h1_ref[...], w_qkv[:, lane : lane + model_width]
            )
        first = lengths_ref[0, 0]
        both = first + lengths_ref[0, 1]

        def segment(axis):
            slot = lax.broadcasted_iota(jnp.int32, (slots, slots), axis)
            return (slot >= first).astype(jnp.int32) + (slot >= both).astype(jnp.int32)

        allowed = segment(0) == segment(1)
        cosine_rows, sine_rows = cosine_ref[...], sine_ref[...]
        for lane in range(0, model_width, LANES):
            block = slice(lane, lane + LANES)

            def rope(offset):
                raw = joined[:, offset + lane : offset + lane + LANES]
                return turn_halves(raw, cosine_rows, sine_rows)

            query = (rope(0) * HEAD ** (-0.5)).astype(BF16)
            key = rope(model_width).astype(BF16)
            value = joined[:, 2 * model_width + lane : 2 * model_width + lane + LANES].astype(BF16)
            q_ref[:, block] = query
            k_ref[:, block] = key
            v_ref[:, block] = value
            context = None
            for head in range(2):
                scores = jnp.where(allowed, dot_nt(only(query, head), key), MASK_FILL)
                exponent = jnp.exp(scores - jnp.max(scores, -1, keepdims=True))
                total = jnp.sum(exponent, -1, keepdims=True)
                probs = (exponent * (1.0 / total)).astype(BF16)
                probs_ref[lane // HEAD + head] = probs
                part = dot_nn(probs, only(value, head))
                context = part if context is None else context + part
            context_ref[:, block] = context.astype(BF16)
        middle = inputs + dot_nn(context_ref[...], w_out[...])
        middle_ref[...] = middle
        h2_ref[...] = (normalised(middle)[0] * gain_rows[1:2, :]).astype(BF16)

    wide = (slots, model_width)
    return run_kernel(
        body,
        "attention_forward",
        [(wide, BF16)] * 4
        + [((model_width // HEAD, slots, slots), BF16), (wide, BF16), (wide, F32), (wide, BF16)]
        + [((model_width, qkv_width), BF16), ((model_width, out_width), BF16)]
        + [((8, model_width), F32)],
        [pltpu.VMEM((model_width, LANES), BF16), pltpu.VMEM((slots, qkv_width), F32)],
        [lengths, tokens, cosine, sine, *pieces],
        scalars=1,
    )


ERF_UP = (0.00022905065861350646, 0.0034082910107109506, 0.050955695062380861,
          0.18520832239976145, 1.128379143519084)
ERF_DOWN = (-1.1791602954361697e-7, 0.000023547966471313185, 0.0010179625278914885,
            0.014070470171167667, 0.11098505178285362, 0.49746925110067538, 1.0)


def erf(values):
    values = jnp.clip(values, -3.832506856900711, 3.832506856900711)
    square = values * values
    up = jnp.full_like(values, ERF_UP[0])
    for term in ERF_UP[1:]:
        up = up * square + term
    down = jnp.full_like(values, ERF_DOWN[0])
    for term in ERF_DOWN[1:]:
        down = down * square + term
    return values * up / down


def feed_forward(h2, cotangent, pieces, in_width, ff_width):
    slots, model_width = h2.shape
    count = len(pieces)
    outs = grad_outs(model_width, ff_width)
    scratch = grad_scratch(model_width, slots)

    def body(*refs):
        h2_ref, cotangent_ref = refs[:2]
        piece_refs = refs[2 : 2 + count]
        mixed_ref, grad_hidden_ref, w_in, w_down_t = refs[2 + count : 6 + count]
        grad_refs = refs[6 + count : 6 + count + len(outs)]
        turning = refs[6 + count + len(outs) :]
        lay_out(piece_refs, [w_in, w_down_t])
        grad_out = cotangent_ref[...].astype(BF16)
        for lane in range(0, ff_width, STEP):
            here, there = slice(lane, lane + STEP), slice(ff_width + lane, ff_width + lane + STEP)
            raw = dot_nn(h2_ref[...], w_in[:, here])
            gate = dot_nn(h2_ref[...], w_in[:, there])
            grad_mixed = dot_nn(grad_out, w_down_t[:, here])
            below = 0.5 * (1.0 + erf(raw * 0.7071067811865476))
            bell = jnp.exp(raw * raw * -0.5) * 0.3989422804014327
            active = raw * below
            mixed_ref[:, here] = (active * gate).astype(BF16)
            grad_hidden_ref[:, here] = (grad_mixed * gate * (below + raw * bell)).astype(BF16)
            grad_hidden_ref[:, there] = (grad_mixed * active).astype(BF16)
        write_weight_grad(cotangent_ref[...], mixed_ref, grad_refs, turning)

    results = run_kernel(
        body,
        "feed_forward",
        [((slots, ff_width), BF16), ((slots, in_width), BF16)]
        + [((model_width, in_width), BF16), ((model_width, ff_width), BF16)]
        + outs,
        scratch,
        [h2, cotangent, *pieces],
    )
    return results[:4], results[4:]


def weight_grad(rows_side, columns_side):
    slots, model_width = rows_side.shape
    outs = grad_outs(model_width, columns_side.shape[1])

    def body(rows_ref, columns_ref, *refs):
        write_weight_grad(rows_ref[...], columns_ref, refs[: len(outs)], refs[len(outs) :])

    return run_kernel(
        body, "weight_grad", outs, grad_scratch(model_width, slots), [rows_side, columns_side]
    )


def middle_backward(grad_hidden, w_in, middle, gains, cotangent, w_out, context):
    slots, model_width = middle.shape
    outs = grad_outs(model_width, w_out.shape[1])

    def body(grad_hidden_ref, w_in_ref, middle_ref, gains_ref, cotangent_ref, w_out_ref,
             context_ref, grad_middle_ref, grad_context_ref, *refs):
        grad_h2 = dot_nt(grad_hidden_ref[...], w_in_ref[...])
        xhat, scale = normalised(middle_ref[...])
        grad_middle = cotangent_ref[...] + norm_back(grad_h2, xhat, scale, gains_ref[1:2, :])
        grad_middle_ref[...] = grad_middle
        narrow = grad_middle.astype(BF16)
        grad_context_ref[...] = dot_nt(narrow, w_out_ref[...]).astype(BF16)
        write_weight_grad(
            context_ref[...], narrow, refs[: len(outs)], refs[len(outs) :]
        )

    wide = (slots, model_width)
    results = run_kernel(
        body,
        "middle_backward",
        [(wide, F32), (wide, BF16)] + outs,
        grad_scratch(model_width, slots),
        [grad_hidden, w_in, middle, gains, cotangent, w_out, context],
    )
    return results[:2], results[2:]


def attention_backward(query, key, value, probs, context, grad_context, cosine, sine, h1):
    slots, model_width = query.shape
    outs = grad_outs(model_width, 3 * model_width)

    def body(q_ref, k_ref, v_ref, probs_ref, context_ref, grad_context_ref, cosine_ref, sine_ref,
             h1_ref, joined_ref, *refs):
        cosine_rows, sine_rows = cosine_ref[...], -sine_ref[...]
        for lane in range(0, model_width, LANES):
            block = slice(lane, lane + LANES)
            query, key, value = q_ref[:, block], k_ref[:, block], v_ref[:, block]
            grad = grad_context_ref[:, block]
            product = grad.astype(F32) * context_ref[:, block].astype(F32)
            grad_query = grad_key = grad_value = 0.0
            for head in range(2):
                here = probs_ref[lane // HEAD + head]
                inner = jnp.sum(only(product, head), -1, keepdims=True)
                grad_probs = dot_nt(only(grad, head), value)
                grad_scores = (here.astype(F32) * (grad_probs - inner)).astype(BF16)
                grad_value += dot_tn(only(grad, head), here)
                grad_query += dot_nn(grad_scores, only(key, head))
                grad_key += dot_tn(only(query, head), grad_scores)
            grad_query = turn_halves(grad_query * HEAD ** (-0.5), cosine_rows, sine_rows)
            grad_key = turn_halves(grad_key.T, cosine_rows, sine_rows)
            joined_ref[:, block] = grad_query.astype(BF16)
            joined_ref[:, model_width + lane : model_width + lane + LANES] = grad_key.astype(BF16)
            joined_ref[:, 2 * model_width + lane : 2 * model_width + lane + LANES] = (
                grad_value.T.astype(BF16)
            )
        write_weight_grad(h1_ref[...], joined_ref, refs[: len(outs)], refs[len(outs) :])

    results = run_kernel(
        body,
        "attention_backward",
        [((slots, 3 * model_width), BF16)] + outs,
        grad_scratch(model_width, slots),
        [query, key, value, probs, context, grad_context, cosine, sine, h1],
    )
    return results[0], results[1:]


def finish(tokens, middle, mixed, w_down_t, grad_joined, w_qkv, grad_middle, gains):
    def body(tokens_ref, middle_ref, mixed_ref, w_down_ref, joined_ref, w_qkv_ref,
             grad_middle_ref, gains_ref, output_ref, grad_ref):
        output = middle_ref[...] + dot_nt(mixed_ref[...], w_down_ref[...])
        output_ref[...] = output.astype(BF16)
        grad_h1 = dot_nt(joined_ref[...], w_qkv_ref[...])
        xhat, scale = normalised(tokens_ref[...].astype(F32))
        grad_ref[...] = grad_middle_ref[...] + norm_back(grad_h1, xhat, scale, gains_ref[0:1, :])

    return run_kernel(
        body,
        "finish",
        [(tokens.shape, BF16), (tokens.shape, F32)],
        [],
        [tokens, middle, mixed, w_down_t, grad_joined, w_qkv, grad_middle, gains],
    )


def add(*parts):
    return sum(part.astype(F32) for part in parts).astype(BF16)


def scatter_sum(parts):
    if len(parts) == 1:
        return lax.psum_scatter(parts[0], "fsdp", scatter_dimension=0, tiled=True).astype(F32)
    keep, send = parts
    half = keep.shape[0] // 8
    other = swap(send, CORE)

    def chip(first, count):
        rows = slice(first * half, (first + count) * half)
        return add(keep[rows], other[rows])

    by_x = swap(chip(0, 2), ALONG_X)
    by_y = swap(chip(2, 2), ALONG_Y)
    late_x = swap(add(keep[4 * half : 5 * half], other[4 * half : 5 * half], by_y[:half]), ALONG_X)
    late_y = swap(add(keep[5 * half : 6 * half], other[5 * half : 6 * half], by_x[:half]), ALONG_Y)
    own = keep[6 * half :].astype(F32) + other[6 * half :].astype(F32)
    own += jnp.concatenate([by_x[half:], by_y[half:]], 0).astype(F32)
    own += jnp.concatenate([late_y, late_x], 0).astype(F32)
    return own


def copies_sum(values):
    copies = lax.axis_size("replica")
    me = lax.axis_index("replica")
    rows, width = values.shape
    part = rows // copies
    narrow = values.astype(BF16)

    def shift(array, by):
        return lax.ppermute(array, "replica", [(i, (i + by) % copies) for i in range(copies)])

    def part_of(array, at):
        return lax.dynamic_slice_in_dim(array, at * part, part, 0)

    total = part_of(values, me)
    for by in range(1, copies):
        total += shift(part_of(narrow, (me + by) % copies), by).astype(F32)
    total = total.astype(BF16)
    result = jnp.zeros((copies, part, width), BF16)
    result = lax.dynamic_update_index_in_dim(result, total, me, 0)
    for by in range(1, copies):
        result = lax.dynamic_update_index_in_dim(
            result, shift(total, by), (me + copies - by) % copies, 0
        )
    return result.reshape(rows, width).astype(F32)


def per_device(
    tokens,
    seq_lengths,
    norm1_gain,
    qkv_weight,
    out_weight,
    norm2_gain,
    in_weight,
    down_weight,
    cotangent,
):
    slot_count = tokens.shape[0]
    qkv_width, out_width = qkv_weight.shape[1], out_weight.shape[1]
    in_width, ff_width = in_weight.shape[1], down_weight.shape[0]
    gain_columns = jnp.pad(jnp.stack([norm1_gain, norm2_gain], 1), ((0, 0), (0, LANES - 2)))
    attn_pieces = gathered(jnp.concatenate([qkv_weight, out_weight, gain_columns], 1))
    mlp_pieces = gathered(jnp.concatenate([in_weight, down_weight.T], 1))
    positions = slot_layout(seq_lengths, slot_count)[1][0]
    cosine, sine = rope_tables(positions, HEAD)
    cosine = jnp.concatenate([cosine] * 4, 1)
    sine = jnp.concatenate([-sine, sine, -sine, sine], 1)

    (h1, query, key, value, probs, context, middle, h2, w_qkv, w_out, gains) = attention_forward(
        seq_lengths, tokens, cosine, sine, attn_pieces, qkv_width, out_width
    )
    (mixed, grad_hidden, w_in, w_down_t), down_parts = feed_forward(
        h2, cotangent, mlp_pieces, in_width, ff_width
    )
    down_shard = scatter_sum(down_parts)
    in_shard = scatter_sum(weight_grad(h2, grad_hidden))
    (grad_middle, grad_context), out_parts = middle_backward(
        grad_hidden, w_in, middle, gains, cotangent, w_out, context
    )
    out_shard = scatter_sum(out_parts)
    grad_joined, qkv_parts = attention_backward(
        query, key, value, probs, context, grad_context, cosine, sine, h1
    )
    qkv_shard = scatter_sum(qkv_parts)
    output, grad_tokens = finish(
        tokens, middle, mixed, w_down_t, grad_joined, w_qkv, grad_middle, gains
    )
    mlp_sum = copies_sum(jnp.concatenate([in_shard, down_shard], 1))
    attn_sum = copies_sum(jnp.concatenate([qkv_shard, out_shard], 1))
    grad_qkv, grad_out = attn_sum[:, :qkv_width], attn_sum[:, qkv_width:]
    grad_in, grad_down = mlp_sum[:, :in_width], mlp_sum[:, in_width:].T

    def gain_grad(weight, weight_sum, gain):
        return jnp.sum(weight.astype(F32) * weight_sum, 1) / gain.astype(F32)

    return (
        output,
        grad_tokens,
        gain_grad(qkv_weight, grad_qkv, norm1_gain),
        grad_qkv,
        grad_out,
        gain_grad(in_weight, grad_in, norm2_gain),
        grad_in,
        grad_down,
    )


def solution(mesh):
    return jax.shard_map(
        per_device,
        mesh=mesh,
        in_specs=(
            P(("replica", "fsdp"), None),
            P(("replica", "fsdp"), None),
            P("fsdp"),
            P("fsdp", None),
            P("fsdp", None),
            P("fsdp"),
            P("fsdp", None),
            P(None, "fsdp"),
            P(("replica", "fsdp"), None),
        ),
        out_specs=(
            P(("replica", "fsdp"), None),
            P(("replica", "fsdp"), None),
            P("fsdp"),
            P("fsdp", None),
            P("fsdp", None),
            P("fsdp"),
            P("fsdp", None),
            P(None, "fsdp"),
        ),
        check_vma=False,
    )
```

time: 528 us -> 211 us (0.40)
  Pallas kernels: 317 us -> 37.3 us
  matrix products: 29.1 us -> 0 us
  local copies, waits for them, and re-layouts: 23.5 us -> 16.7 us
  starting transfers between devices: 57.7 us -> 64 us
    pallas_call x6, Pallas kernels: 317 us -> 37.3 us  [run_kernel(): pl.pallas_call(body, out_shape=[jax.ShapeDtypeStruct(shape, kind) for sha...]
    dot_general x13 -> x0, matrix products: 25.2 us -> none  [the longest x1 3.43 us: per_device(): jnp.einsum('td,df->tf', grad_out_b, w_down_t, preferred_element_type=jnp....]
    unnamed x118 -> x80, local copies, waits for them, and re-layouts: 6.67 us -> 13.9 us
    ppermute x12, starting transfers between devices: 27.7 us -> 34.5 us  [shift(): lax.ppermute(array, 'replica', [(i, (i + by) % copies) for i in range(cop...]
    convert_element_type x8, other arithmetic: 1.04 us -> 7.2 us  [add(): return sum((part.astype(F32) for part in parts)).astype(BF16)]
    reshape x3 -> x0, local copies, waits for them, and re-layouts: 5.74 us -> none  [the longest x1 1.92 us: per_device(): raw_grads[0].reshape(slot_count, model_width)]
    ppermute x12, waiting for transfers between devices: 16.6 us -> 10.8 us  [shift(): lax.ppermute(array, 'replica', [(i, (i + by) % copies) for i in range(cop...]
  transfers between devices with their start and end apart: 50 -> 50, of which waited for: 24 -> 18; matrix products, arithmetic and copies ran while one was open for 6% -> 8% of each run, Pallas kernels for 29% -> 14%
where the time goes in v2:
time: 211 us; the launch traced here: 210 us
  waiting for transfers between devices  72 us (34%)
  starting transfers between devices  64 us (30%)
  Pallas kernels  37.3 us (18%)
  other arithmetic  17.5 us (8%)
  local copies, waits for them, and re-layouts  16.7 us (8%)
  between operations  2.5 us (1%)
    ppermute x38, waiting for transfers between devices, swap(): return lax.ppermute(values, 'fsdp', [(i, i ^ mask) for i in range(8)])  61.2 us
    pallas_call x6, Pallas kernels, run_kernel(): pl.pallas_call(body, out_shape=[jax.ShapeDtypeStruct(shape, kind) for sha...  37.3 us
    ppermute x12, starting transfers between devices, shift(): lax.ppermute(array, 'replica', [(i, (i + by) % copies) for i in range(cop...  34.5 us
    ppermute x38, starting transfers between devices, swap(): return lax.ppermute(values, 'fsdp', [(i, i ^ mask) for i in range(8)])  29.5 us
    unnamed x80, local copies, waits for them, and re-layouts  13.9 us
    ppermute x12, waiting for transfers between devices, shift(): lax.ppermute(array, 'replica', [(i, (i + by) % copies) for i in range(cop...  10.8 us
    convert_element_type x8, other arithmetic, add(): return sum((part.astype(F32) for part in parts)).astype(BF16)  7.2 us
  transfers between devices with their start and end apart: 50, of which 18 were waited for; matrix products, arithmetic and copies ran while one was open for 8% of the time, Pallas kernels for 14%

profile of v2, /device:TPU:0, one launch (start us, length us, event | category | flops | bytes accessed | tf_op | source)
XLA Modules:
  0.0 209.9 jit_solution(5582714032600379783)
XLA Ops:
  1.9 3.0 %collective-permute-start.10 = (bf16[96,3456]{1,0:T(8,128)(2,1)S(1)}, bf16[96,3456]{1,0:T(8,128)(2,1)S(1)}, u32[]{:S(2)}, u32[]{:S(2)}) collective-permute-start(bf16[96,3456]{1,0:T(8,128)(2,1)S(1)} %pad_maximum_fusion.2.refs_2_), channel_id=1, source_target_pairs={{0,4},{1,5},{2,6},{3,7},{4,0},{5,1},{6,2},{7,3},{8,12},{9,13},{10,... | collective-permute-start | bytes 1990664 | tf_op jit(solution)/shard_map/ppermute | solution.py:56
  5.3 2.0 collective-permute-start
  7.3 25.7 %collective-permute-done.1.refs_6_ = bf16[96,3200]{1,0:T(8,128)(2,1)S(1)} collective-permute-done((bf16[96,3200]{1,0:T(8,128)(2,1)S(1)}, bf16[96,3200]{1,0:T(8,128)(2,1)S(1)}, u32[]{:S(2)}, u32[]{:S(2)}) %collective-permute-start.1) | collective-permute-done | bytes 614432 | tf_op jit(solution)/shard_map/ppermute | solution.py:56
  33.0 1.8 collective-permute-start.2
  37.5 5.9 %collective-permute-done.2.refs_7_ = bf16[48,3200]{1,0:T(8,128)(2,1)S(1)} collective-permute-done((bf16[48,3200]{1,0:T(8,128)(2,1)S(1)}, bf16[48,3200]{1,0:T(8,128)(2,1)S(1)}, u32[]{:S(2)}, u32[]{:S(2)}) %collective-permute-start.2) | collective-permute-done | bytes 307232 | tf_op jit(solution)/shard_map/ppermute | solution.py:56
  43.3 1.8 collective-permute-done.3.refs_8_
  45.7 3.0 %collective-permute-done.11.refs_5_ = bf16[48,3456]{1,0:T(8,128)(2,1)S(1)} collective-permute-done((bf16[48,3456]{1,0:T(8,128)(2,1)S(1)}, bf16[48,3456]{1,0:T(8,128)(2,1)S(1)}, u32[]{:S(2)}, u32[]{:S(2)}) %collective-permute-start.11) | collective-permute-done | bytes 331808 | tf_op jit(solution)/shard_map/ppermute | solution.py:56
  54.5 10.9 %attention_forward.1 = (bf16[256,768]{1,0:T(8,128)(2,1)S(1)}, bf16[256,768]{1,0:T(8,128)(2,1)S(1)}, bf16[256,768]{1,0:T(8,128)(2,1)S(1)}, bf16[256,768]{1,0:T(8,...) custom-call(s32[1,2]{1,0:T(1,128)S(1)} %copy-done.25, ...), custom_call_target="tpu_custom_call" | custom-call | tf_op jit(solution)/shard_map/attention_forward/pallas_call | solution.py:43
  69.0 8.3 %feed_forward.1 = (bf16[256,1152]{1,0:T(8,128)(2,1)S(1)}, bf16[256,2304]{1,0:T(8,128)(2,1)}, bf16[768,2304]{1,0:T(8,128)(2,1)}, bf16[768,1152]{1,0:T(8,128)(2,1)...) custom-call(bf16[256,768]{1,0:T(8,128)(2,1)S(1)} %get-tuple-element.37.refs_0_.rows_ref, ...), custom_call_target="tpu_custom_call" | custom-call | tf_op jit(solution)/shard_map/feed_forward/pallas_call | solution.py:43
  79.8 6.2 %middle_backward.1 = (f32[256,768]{1,0:T(8,128)S(1)}, bf16[256,768]{1,0:T(8,128)(2,1)S(1)}, bf16[384,768]{1,0:T(8,128)(2,1)S(1)}, bf16[384,768]{1,0:T(8,128)(2,1)}) custom-call(bf16[256,2304]{1,0:T(8,128)(2,1)S(1)} %copy-done, bf16[768,2304]{1,0:T(8,128)(2,1)} %get-tuple-element.46.w_in_ref, f32[256,768]{1,0:T(8,128)S(1)} %copy-done.3, ...), custom_call_target="tpu_custom_call" | custom-call | tf_op jit(solution)/shard_map/middle_backward/pallas_call | solution.py:43
  95.6 5.5 %attention_backward.1 = (bf16[256,2304]{1,0:T(8,128)(2,1)S(1)}, bf16[384,2304]{1,0:T(8,128)(2,1)}, bf16[384,2304]{1,0:T(8,128)(2,1)}) custom-call(bf16[256,768]{1,0:T(8,128)(2,1)S(1)} %copy-done.18, bf16[256,768]{1,0:T(8,128)(2,1)S(1)} %copy-done.20, bf16[256,768]{1,0:T(8,128)(2,1)S(1)} %copy-done.22, bf16[12,256,256]{2,1,0:T(8,128)(2,1)S(1)} %copy-done.6, ...), custom_call_target="tpu_custom_call" | custom-call | tf_op jit(solution)/shard_map/attention_backward/pallas_call | solution.py:43
  101.2 4.9 %finish.1 = (bf16[256,768]{1,0:T(8,128)(2,1)}, f32[256,768]{1,0:T(8,128)}) custom-call(bf16[256,768]{1,0:T(8,128)(2,1)S(1)} %copy-done.5, f32[256,768]{1,0:T(8,128)S(1)} %copy-done.3, bf16[256,1152]{1,0:T(8,128)(2,1)S(1)} %copy-done.12, bf16[768,1152]{1,0:T(8,128)(2,1)S(1)} %copy-done.4, bf16[256,2304]{1,0:T(8,128)(2,1)S(1)} %get-tuple-element.51.joined_ref, ...), custom_call_target="tpu_custom_call" | custom-call | tf_op jit(solution)/shard_map/finish/pallas_call | solution.py:43
  112.0 1.8 collective-permute-done.24
  119.2 2.0 collective-permute-done.41
  125.3 1.7 collective-permute-done.42
  135.4 8.8 %collective-permute-done.19 = bf16[96,2304]{1,0:T(8,128)(2,1)S(1)} collective-permute-done((bf16[96,2304]{1,0:T(8,128)(2,1)S(1)}, bf16[96,2304]{1,0:T(8,128)(2,1)S(1)}, u32[]{:S(2)}, u32[]{:S(2)}) %collective-permute-start.19) | collective-permute-done | bytes 442400 | tf_op jit(solution)/shard_map/ppermute | solution.py:56
  148.0 5.4 %collective-permute-done.35 = bf16[96,2304]{1,0:T(8,128)(2,1)S(1)} collective-permute-done((bf16[96,2304]{1,0:T(8,128)(2,1)S(1)}, bf16[96,2304]{1,0:T(8,128)(2,1)S(1)}, u32[]{:S(2)}, u32[]{:S(2)}) %collective-permute-start.35) | collective-permute-done | bytes 442400 | tf_op jit(solution)/shard_map/ppermute | solution.py:56
  159.4 2.6 %collective-permute-start.29 = (bf16[24,3072]{1,0:T(8,128)(2,1)S(1)}, bf16[24,3072]{1,0:T(8,128)(2,1)S(1)}, u32[]{:S(2)}, u32[]{:S(2)}) collective-permute-start(bf16[24,3072]{1,0:T(8,128)(2,1)S(1)} %get-tuple-element.93), channel_id=1, source_target_pairs={{0,16},{8,24},{16,0},{24,8},{1,17},{9,25},{17,1},{25,9},{2,18},{10... | collective-permute-start | bytes 442376 | tf_op jit(solution)/shard_map/ppermute | solution.py:444
  167.6 4.4 %collective-permute-done.29 = bf16[24,3072]{1,0:T(8,128)(2,1)S(1)} collective-permute-done((bf16[24,3072]{1,0:T(8,128)(2,1)S(1)}, bf16[24,3072]{1,0:T(8,128)(2,1)S(1)}, u32[]{:S(2)}, u32[]{:S(2)}) %collective-permute-start.29) | collective-permute-done | bytes 147488 | tf_op jit(solution)/shard_map/ppermute | solution.py:444
  172.1 9.3 %collective-permute-start.31 = (bf16[24,3072]{1,0:T(8,128)(2,1)S(1)}, bf16[24,3072]{1,0:T(8,128)(2,1)S(1)}, u32[]{:S(2)}, u32[]{:S(2)}) collective-permute-start(bf16[24,3072]{1,0:T(8,128)(2,1)S(1)} %get-tuple-element.71), channel_id=1, source_target_pairs={{0,8},{8,16},{16,24},{24,0},{1,9},{9,17},{17,25},{25,1},{2,10},{10... | collective-permute-start | bytes 442376 | tf_op jit(solution)/shard_map/ppermute | solution.py:444
  181.4 3.4 %collective-permute-start.32 = (bf16[24,3072]{1,0:T(8,128)(2,1)S(1)}, bf16[24,3072]{1,0:T(8,128)(2,1)S(1)}, u32[]{:S(2)}, u32[]{:S(2)}) collective-permute-start(bf16[24,3072]{1,0:T(8,128)(2,1)S(1)} %get-tuple-element.71), channel_id=1, source_target_pairs={{0,16},{8,24},{16,0},{24,8},{1,17},{9,25},{17,1},{25,9},{2,18},{10... | collective-permute-start | bytes 442376 | tf_op jit(solution)/shard_map/ppermute | solution.py:444
  185.0 10.3 %collective-permute-start.47 = (bf16[24,3456]{1,0:T(8,128)(2,1)S(1)}, bf16[24,3456]{1,0:T(8,128)(2,1)S(1)}, u32[]{:S(2)}, u32[]{:S(2)}) collective-permute-start(bf16[24,3456]{1,0:T(8,128)(2,1)S(1)} %get-tuple-element.67), channel_id=1, source_target_pairs={{0,8},{8,16},{16,24},{24,0},{1,9},{9,17},{17,25},{25,1},{2,10},{10... | collective-permute-start | bytes 497672 | tf_op jit(solution)/shard_map/ppermute | solution.py:444
  195.3 3.4 %collective-permute-start.48 = (bf16[24,3456]{1,0:T(8,128)(2,1)S(1)}, bf16[24,3456]{1,0:T(8,128)(2,1)S(1)}, u32[]{:S(2)}, u32[]{:S(2)}) collective-permute-start(bf16[24,3456]{1,0:T(8,128)(2,1)S(1)} %get-tuple-element.67), channel_id=1, source_target_pairs={{0,16},{8,24},{16,0},{24,8},{1,17},{9,25},{17,1},{25,9},{2,18},{10... | collective-permute-start | bytes 497672 | tf_op jit(solution)/shard_map/ppermute | solution.py:444
  202.1 5.2 %collective-permute-done.48 = bf16[24,3456]{1,0:T(8,128)(2,1)S(1)} collective-permute-done((bf16[24,3456]{1,0:T(8,128)(2,1)S(1)}, bf16[24,3456]{1,0:T(8,128)(2,1)S(1)}, u32[]{:S(2)}, u32[]{:S(2)}) %collective-permute-start.48) | collective-permute-done | bytes 165920 | tf_op jit(solution)/shard_map/ppermute | solution.py:444
  (219 shorter events, 70.4 us)
Async XLA Ops:
  1.9 34.5 %collective-permute-start.10 = (bf16[96,3456]{1,0:T(8,128)(2,1)S(1)}, bf16[96,3456]{1,0:T(8,128)(2,1)S(1)}, u32[]{:S(2)}, u32[]{:S(2)}) collective-permute-start(bf16[96,3456]{1,0:T(8,128)(2,1)S(1)} %pad_maximum_fusion.2.refs_2_), channel_id=1, source_target_pairs={{0,4},{1,5},{2,6},{3,7},{4,0},{5,1},{6,2},{7,3},{8,12},{9,13},{10,... | collective-permute-start | bytes 1990664 | tf_op jit(solution)/shard_map/ppermute | solution.py:56
  5.2 27.9 %collective-permute-start.1 = (bf16[96,3200]{1,0:T(8,128)(2,1)S(1)}, bf16[96,3200]{1,0:T(8,128)(2,1)S(1)}, u32[]{:S(2)}, u32[]{:S(2)}) collective-permute-start(bf16[96,3200]{1,0:T(8,128)(2,1)S(1)} %fusion.3.refs_4_), channel_id=1, source_target_pairs={{0,4},{1,5},{2,6},{3,7},{4,0},{5,1},{6,2},{7,3},{8,12},{9,13},{10,... | collective-permute-start | bytes 1843208 | tf_op jit(solution)/shard_map/ppermute | solution.py:56
  5.3 29.6 %collective-permute-start = (bf16[96,3200]{1,0:T(8,128)(2,1)S(1)}, bf16[96,3200]{1,0:T(8,128)(2,1)S(1)}, u32[]{:S(2)}, u32[]{:S(2)}) collective-permute-start(bf16[96,3200]{1,0:T(8,128)(2,1)S(1)} %fusion.3.refs_4_), channel_id=1, source_target_pairs={{0,2},{1,3},{2,0},{3,1},{4,6},{5,7},{6,4},{7,5},{8,10},{9,11},{10,... | collective-permute-start | bytes 1843208 | tf_op jit(solution)/shard_map/ppermute | solution.py:56
  7.2 29.9 %collective-permute-start.9 = (bf16[96,3456]{1,0:T(8,128)(2,1)S(1)}, bf16[96,3456]{1,0:T(8,128)(2,1)S(1)}, u32[]{:S(2)}, u32[]{:S(2)}) collective-permute-start(bf16[96,3456]{1,0:T(8,128)(2,1)S(1)} %pad_maximum_fusion.2.refs_2_), channel_id=1, source_target_pairs={{0,2},{1,3},{2,0},{3,1},{4,6},{5,7},{6,4},{7,5},{8,10},{9,11},{10,... | collective-permute-start | bytes 1990664 | tf_op jit(solution)/shard_map/ppermute | solution.py:56
  7.3 37.8 %collective-permute-start.4 = (bf16[96,3200]{1,0:T(8,128)(2,1)S(1)}, bf16[96,3200]{1,0:T(8,128)(2,1)S(1)}, u32[]{:S(2)}, u32[]{:S(2)}) collective-permute-start(bf16[96,3200]{1,0:T(8,128)(2,1)S(1)} %fusion.3.refs_4_), channel_id=1, source_target_pairs={{0,1},{1,0},{2,3},{3,2},{4,5},{5,4},{6,7},{7,6},{8,9},{9,8},{10,11... | collective-permute-start | bytes 1843208 | tf_op jit(solution)/shard_map/ppermute | solution.py:56
  49.9 17.0 %collective-permute-start.13 = (bf16[96,3456]{1,0:T(8,128)(2,1)S(1)}, bf16[96,3456]{1,0:T(8,128)(2,1)S(1)}, u32[]{:S(2)}, u32[]{:S(2)}) collective-permute-start(bf16[96,3456]{1,0:T(8,128)(2,1)S(1)} %pad_maximum_fusion.2.refs_2_), channel_id=1, source_target_pairs={{0,1},{1,0},{2,3},{3,2},{4,5},{5,4},{6,7},{7,6},{8,9},{9,8},{10,11... | collective-permute-start | bytes 1990664 | tf_op jit(solution)/shard_map/ppermute | solution.py:56
  49.9 17.0 %collective-permute-start.14 = (bf16[96,3456]{1,0:T(8,128)(2,1)S(1)}, bf16[96,3456]{1,0:T(8,128)(2,1)S(1)}, u32[]{:S(2)}, u32[]{:S(2)}) collective-permute-start(bf16[96,3456]{1,0:T(8,128)(2,1)S(1)} %collective-permute-done.9.refs_3_), channel_id=1, source_target_pairs={{0,1},{1,0},{2,3},{3,2},{4,5},{5,4},{6,7},{7,6},{8,9},{9,8},{10,11... | collective-permute-start | bytes 1990664 | tf_op jit(solution)/shard_map/ppermute | solution.py:56
  50.4 16.5 %collective-permute-start.15 = (bf16[96,3456]{1,0:T(8,128)(2,1)S(1)}, bf16[96,3456]{1,0:T(8,128)(2,1)S(1)}, u32[]{:S(2)}, u32[]{:S(2)}) collective-permute-start(bf16[96,3456]{1,0:T(8,128)(2,1)S(1)} %collective-permute-done.10.refs_4_), channel_id=1, source_target_pairs={{0,1},{1,0},{2,3},{3,2},{4,5},{5,4},{6,7},{7,6},{8,9},{9,8},{10,11... | collective-permute-start | bytes 1990664 | tf_op jit(solution)/shard_map/ppermute | solution.py:56
  53.1 13.9 %collective-permute-start.16 = (bf16[48,3456]{1,0:T(8,128)(2,1)S(1)}, bf16[48,3456]{1,0:T(8,128)(2,1)S(1)}, u32[]{:S(2)}, u32[]{:S(2)}) collective-permute-start(bf16[48,3456]{1,0:T(8,128)(2,1)S(1)} %collective-permute-done.11.refs_5_), channel_id=1, source_target_pairs={{0,1},{1,0},{2,3},{3,2},{4,5},{5,4},{6,7},{7,6},{8,9},{9,8},{10,11... | collective-permute-start | bytes 995336 | tf_op jit(solution)/shard_map/ppermute | solution.py:56
  53.6 13.4 %collective-permute-start.17 = (bf16[48,3456]{1,0:T(8,128)(2,1)S(1)}, bf16[48,3456]{1,0:T(8,128)(2,1)S(1)}, u32[]{:S(2)}, u32[]{:S(2)}) collective-permute-start(bf16[48,3456]{1,0:T(8,128)(2,1)S(1)} %collective-permute-done.12.refs_6_), channel_id=1, source_target_pairs={{0,1},{1,0},{2,3},{3,2},{4,5},{5,4},{6,7},{7,6},{8,9},{9,8},{10,11... | collective-permute-start | bytes 995336 | tf_op jit(solution)/shard_map/ppermute | solution.py:56
  78.1 31.4 %collective-permute-start.39 = (bf16[384,1152]{1,0:T(8,128)(2,1)}, bf16[384,1152]{1,0:T(8,128)(2,1)}, u32[]{:S(2)}, u32[]{:S(2)}) collective-permute-start(bf16[384,1152]{1,0:T(8,128)(2,1)} %get-tuple-element.63), channel_id=1, source_target_pairs={{0,1},{1,0},{2,3},{3,2},{4,5},{5,4},{6,7},{7,6},{8,9},{9,8},{10,11... | collective-permute-start | bytes 2654216 | tf_op jit(solution)/shard_map/ppermute | solution.py:56
  88.5 17.6 %collective-permute-start.23 = (bf16[384,768]{1,0:T(8,128)(2,1)}, bf16[384,768]{1,0:T(8,128)(2,1)}, u32[]{:S(2)}, u32[]{:S(2)}) collective-permute-start(bf16[384,768]{1,0:T(8,128)(2,1)} %get-tuple-element.59), channel_id=1, source_target_pairs={{0,1},{1,0},{2,3},{3,2},{4,5},{5,4},{6,7},{7,6},{8,9},{9,8},{10,11... | collective-permute-start | bytes 1769480 | tf_op jit(solution)/shard_map/ppermute | solution.py:56
  90.1 42.0 %collective-permute-start.34 = (bf16[384,2304]{1,0:T(8,128)(2,1)S(1)}, bf16[384,2304]{1,0:T(8,128)(2,1)S(1)}, u32[]{:S(2)}, u32[]{:S(2)}) collective-permute-start(bf16[384,2304]{1,0:T(8,128)(2,1)S(1)} %get-tuple-element.61), channel_id=1, source_target_pairs={{0,1},{1,0},{2,3},{3,2},{4,5},{5,4},{6,7},{7,6},{8,9},{9,8},{10,11... | collective-permute-start | bytes 5308424 | tf_op jit(solution)/shard_map/ppermute | solution.py:56
  101.1 28.5 %collective-permute-start.18 = (bf16[384,2304]{1,0:T(8,128)(2,1)}, bf16[384,2304]{1,0:T(8,128)(2,1)}, u32[]{:S(2)}, u32[]{:S(2)}) collective-permute-start(bf16[384,2304]{1,0:T(8,128)(2,1)} %get-tuple-element.57), channel_id=1, source_target_pairs={{0,1},{1,0},{2,3},{3,2},{4,5},{5,4},{6,7},{7,6},{8,9},{9,8},{10,11... | collective-permute-start | bytes 5308424 | tf_op jit(solution)/shard_map/ppermute | solution.py:56
  131.0 13.2 %collective-permute-start.19 = (bf16[96,2304]{1,0:T(8,128)(2,1)S(1)}, bf16[96,2304]{1,0:T(8,128)(2,1)S(1)}, u32[]{:S(2)}, u32[]{:S(2)}) collective-permute-start(bf16[96,2304]{1,0:T(8,128)(2,1)S(1)} %get-tuple-element.78), channel_id=1, source_target_pairs={{0,2},{1,3},{2,0},{3,1},{4,6},{5,7},{6,4},{7,5},{8,10},{9,11},{10,... | collective-permute-start | bytes 1327112 | tf_op jit(solution)/shard_map/ppermute | solution.py:56
  132.3 21.1 %collective-permute-start.35 = (bf16[96,2304]{1,0:T(8,128)(2,1)S(1)}, bf16[96,2304]{1,0:T(8,128)(2,1)S(1)}, u32[]{:S(2)}, u32[]{:S(2)}) collective-permute-start(bf16[96,2304]{1,0:T(8,128)(2,1)S(1)} %get-tuple-element.74), channel_id=1, source_target_pairs={{0,2},{1,3},{2,0},{3,1},{4,6},{5,7},{6,4},{7,5},{8,10},{9,11},{10,... | collective-permute-start | bytes 1327112 | tf_op jit(solution)/shard_map/ppermute | solution.py:56
  133.9 20.1 %collective-permute-start.36 = (bf16[96,2304]{1,0:T(8,128)(2,1)S(1)}, bf16[96,2304]{1,0:T(8,128)(2,1)S(1)}, u32[]{:S(2)}, u32[]{:S(2)}) collective-permute-start(bf16[96,2304]{1,0:T(8,128)(2,1)S(1)} %get-tuple-element.75), channel_id=1, source_target_pairs={{0,4},{1,5},{2,6},{3,7},{4,0},{5,1},{6,2},{7,3},{8,12},{9,13},{10,... | collective-permute-start | bytes 1327112 | tf_op jit(solution)/shard_map/ppermute | solution.py:56
  163.7 21.1 %collective-permute-start.44 = (bf16[24,3456]{1,0:T(8,128)(2,1)S(1)}, bf16[24,3456]{1,0:T(8,128)(2,1)S(1)}, u32[]{:S(2)}, u32[]{:S(2)}) collective-permute-start(bf16[24,3456]{1,0:T(8,128)(2,1)S(1)} %get-tuple-element.88), channel_id=1, source_target_pairs={{0,8},{8,16},{16,24},{24,0},{1,9},{9,17},{17,25},{25,1},{2,10},{10... | collective-permute-start | bytes 497672 | tf_op jit(solution)/shard_map/ppermute | solution.py:444
  164.4 20.3 %collective-permute-start.45 = (bf16[24,3456]{1,0:T(8,128)(2,1)S(1)}, bf16[24,3456]{1,0:T(8,128)(2,1)S(1)}, u32[]{:S(2)}, u32[]{:S(2)}) collective-permute-start(bf16[24,3456]{1,0:T(8,128)(2,1)S(1)} %get-tuple-element.90), channel_id=1, source_target_pairs={{0,16},{8,24},{16,0},{24,8},{1,17},{9,25},{17,1},{25,9},{2,18},{10... | collective-permute-start | bytes 497672 | tf_op jit(solution)/shard_map/ppermute | solution.py:444
  166.4 18.4 %collective-permute-start.46 = (bf16[24,3456]{1,0:T(8,128)(2,1)S(1)}, bf16[24,3456]{1,0:T(8,128)(2,1)S(1)}, u32[]{:S(2)}, u32[]{:S(2)}) collective-permute-start(bf16[24,3456]{1,0:T(8,128)(2,1)S(1)} %get-tuple-element.89), channel_id=1, source_target_pairs={{0,24},{8,0},{16,8},{24,16},{1,25},{9,1},{17,9},{25,17},{2,26},{10... | collective-permute-start | bytes 497672 | tf_op jit(solution)/shard_map/ppermute | solution.py:444
  172.1 26.6 %collective-permute-start.31 = (bf16[24,3072]{1,0:T(8,128)(2,1)S(1)}, bf16[24,3072]{1,0:T(8,128)(2,1)S(1)}, u32[]{:S(2)}, u32[]{:S(2)}) collective-permute-start(bf16[24,3072]{1,0:T(8,128)(2,1)S(1)} %get-tuple-element.71), channel_id=1, source_target_pairs={{0,8},{8,16},{16,24},{24,0},{1,9},{9,17},{17,25},{25,1},{2,10},{10... | collective-permute-start | bytes 442376 | tf_op jit(solution)/shard_map/ppermute | solution.py:444
  181.4 17.3 %collective-permute-start.32 = (bf16[24,3072]{1,0:T(8,128)(2,1)S(1)}, bf16[24,3072]{1,0:T(8,128)(2,1)S(1)}, u32[]{:S(2)}, u32[]{:S(2)}) collective-permute-start(bf16[24,3072]{1,0:T(8,128)(2,1)S(1)} %get-tuple-element.71), channel_id=1, source_target_pairs={{0,16},{8,24},{16,0},{24,8},{1,17},{9,25},{17,1},{25,9},{2,18},{10... | collective-permute-start | bytes 442376 | tf_op jit(solution)/shard_map/ppermute | solution.py:444
  184.8 14.0 %collective-permute-start.33 = (bf16[24,3072]{1,0:T(8,128)(2,1)S(1)}, bf16[24,3072]{1,0:T(8,128)(2,1)S(1)}, u32[]{:S(2)}, u32[]{:S(2)}) collective-permute-start(bf16[24,3072]{1,0:T(8,128)(2,1)S(1)} %get-tuple-element.71), channel_id=1, source_target_pairs={{0,24},{8,0},{16,8},{24,16},{1,25},{9,1},{17,9},{25,17},{2,26},{10... | collective-permute-start | bytes 442376 | tf_op jit(solution)/shard_map/ppermute | solution.py:444
  185.0 17.1 %collective-permute-start.47 = (bf16[24,3456]{1,0:T(8,128)(2,1)S(1)}, bf16[24,3456]{1,0:T(8,128)(2,1)S(1)}, u32[]{:S(2)}, u32[]{:S(2)}) collective-permute-start(bf16[24,3456]{1,0:T(8,128)(2,1)S(1)} %get-tuple-element.67), channel_id=1, source_target_pairs={{0,8},{8,16},{16,24},{24,0},{1,9},{9,17},{17,25},{25,1},{2,10},{10... | collective-permute-start | bytes 497672 | tf_op jit(solution)/shard_map/ppermute | solution.py:444
  (68 other events, 470.6 us)

commit v3 on v2

--- a/solution.py
+++ b/solution.py
@@ -38,7 +38,7 @@
 STEP = 384
 
 
-def run_kernel(body, name, outs, scratch, operands, scalars=0, flops=0):
+def run_kernel(body, name, outs, scratch, operands, microseconds, scalars=0):
     smem = pl.BlockSpec(memory_space=pltpu.SMEM)
     return pl.pallas_call(
         body,
@@ -46,8 +46,10 @@
         in_specs=[smem] * scalars + [VMEM] * (len(operands) - scalars),
         out_specs=[VMEM] * len(outs),
         scratch_shapes=scratch,
-        compiler_params=pltpu.CompilerParams(vmem_limit_bytes=48 * 2**20),
-        cost_estimate=pl.CostEstimate(flops=flops, bytes_accessed=0, transcendentals=0),
+        compiler_params=pltpu.CompilerParams(vmem_limit_bytes=24 * 2**20),
+        cost_estimate=pl.CostEstimate(
+            flops=int(microseconds * 1e9), bytes_accessed=0, transcendentals=0
+        ),
         name=name,
     )(*operands)
 
@@ -56,14 +58,24 @@
     return lax.ppermute(values, "fsdp", [(i, i ^ mask) for i in range(8)])
 
 
-def gather_pieces(own):
+def after(values, *earlier):
+    return lax.optimization_barrier((values, earlier))[0]
+
+
+def gather_first(own):
+    return [own, swap(own, ALONG_X), swap(own, ALONG_Y), swap(own, CORE)]
+
+
+def gather_second(own, from_x, from_y):
     half = own.shape[0] // 2
-    from_x = swap(own, ALONG_X)
-    from_y = swap(own, ALONG_Y)
-    diag_a = swap(from_y[:half], ALONG_X)
-    diag_b = swap(from_x[half:], ALONG_Y)
-    mine = [own, from_x, from_y, diag_a, diag_b]
-    return mine + [swap(piece, CORE) for piece in mine]
+    return [swap(from_y[:half], ALONG_X), swap(from_x[half:], ALONG_Y)]
+
+
+def gather_third(first, second):
+    own, from_x, from_y, own_core = first
+    return [own, from_x, from_y, *second, own_core] + [
+        swap(piece, CORE) for piece in (from_x, from_y, *second)
+    ]
 
 
 PIECE_PLACES = [
@@ -73,9 +85,7 @@
 ]
 
 
-def gathered(own):
-    if lax.axis_size("fsdp") == 8:
-        return gather_pieces(own)
+def gathered_whole(own):
     return [lax.all_gather(own, "fsdp", axis=0, tiled=True)]
 
 
@@ -113,7 +123,7 @@
             picked[pl.ds((core * 8 + at) * half, half), :] = turned[pl.ds(start, half), :]
 
 
-def write_grad(lhs, columns, outs):
+def write_grad(lhs, columns, outs, base=0):
     width = columns.shape[1]
     for lane in range(0, width, STEP):
         product = jnp.dot(
@@ -121,7 +131,7 @@
         ).astype(BF16)
         row = 0
         for out in outs:
-            out[:, lane : lane + STEP] = product[row : row + out.shape[0]]
+            out[:, base + lane : base + lane + STEP] = product[row : row + out.shape[0]]
             row += out.shape[0]
 
 
@@ -136,9 +146,9 @@
     return [one, one] if lax.axis_size("fsdp") == 8 else [one]
 
 
-def write_weight_grad(rows_side, columns, outs, scratch):
+def write_weight_grad(rows_side, columns, outs, scratch, base=0):
     pick_rows(rows_side, scratch[0], scratch[1] if len(scratch) > 1 else None)
-    write_grad(scratch[-1], columns, outs)
+    write_grad(scratch[-1], columns, outs, base)
 
 
 def dot_nt(a, b):
@@ -250,6 +260,7 @@
         + [((8, model_width), F32)],
         [pltpu.VMEM((model_width, LANES), BF16), pltpu.VMEM((slots, qkv_width), F32)],
         [lengths, tokens, cosine, sine, *pieces],
+        microseconds=11,
         scalars=1,
     )
 
@@ -307,6 +318,7 @@
         + outs,
         scratch,
         [h2, cotangent, *pieces],
+        microseconds=8,
     )
     return results[:4], results[4:]
 
@@ -319,43 +331,43 @@
         write_weight_grad(rows_ref[...], columns_ref, refs[: len(outs)], refs[len(outs) :])
 
     return run_kernel(
-        body, "weight_grad", outs, grad_scratch(model_width, slots), [rows_side, columns_side]
-    )
-
-
-def middle_backward(grad_hidden, w_in, middle, gains, cotangent, w_out, context):
-    slots, model_width = middle.shape
-    outs = grad_outs(model_width, w_out.shape[1])
-
+        body,
+        "weight_grad",
+        outs,
+        grad_scratch(model_width, slots),
+        [rows_side, columns_side],
+        microseconds=1.5,
+    )
+
+
+def middle_backward(grad_hidden, w_in, middle, gains, cotangent, w_out):
     def body(grad_hidden_ref, w_in_ref, middle_ref, gains_ref, cotangent_ref, w_out_ref,
-             context_ref, grad_middle_ref, grad_context_ref, *refs):
+             grad_middle_ref, grad_context_ref):
         grad_h2 = dot_nt(grad_hidden_ref[...], w_in_ref[...])
         xhat, scale = normalised(middle_ref[...])
         grad_middle = cotangent_ref[...] + norm_back(grad_h2, xhat, scale, gains_ref[1:2, :])
         grad_middle_ref[...] = grad_middle
-        narrow = grad_middle.astype(BF16)
-        grad_context_ref[...] = dot_nt(narrow, w_out_ref[...]).astype(BF16)
-        write_weight_grad(
-            context_ref[...], narrow, refs[: len(outs)], refs[len(outs) :]
-        )
-
-    wide = (slots, model_width)
-    results = run_kernel(
+        grad_context_ref[...] = dot_nt(grad_middle.astype(BF16), w_out_ref[...]).astype(BF16)
+
+    return run_kernel(
         body,
         "middle_backward",
-        [(wide, F32), (wide, BF16)] + outs,
-        grad_scratch(model_width, slots),
-        [grad_hidden, w_in, middle, gains, cotangent, w_out, context],
-    )
-    return results[:2], results[2:]
-
-
-def attention_backward(query, key, value, probs, context, grad_context, cosine, sine, h1):
+        [(middle.shape, F32), (middle.shape, BF16)],
+        [],
+        [grad_hidden, w_in, middle, gains, cotangent, w_out],
+        microseconds=5,
+    )
+
+
+def attention_backward(
+    query, key, value, probs, context, grad_context, cosine, sine, h1, grad_middle
+):
     slots, model_width = query.shape
-    outs = grad_outs(model_width, 3 * model_width)
+    outs = grad_outs(model_width, 2 * model_width)
+    scratch = grad_scratch(model_width, slots)
 
     def body(q_ref, k_ref, v_ref, probs_ref, context_ref, grad_context_ref, cosine_ref, sine_ref,
-             h1_ref, joined_ref, *refs):
+             h1_ref, grad_middle_ref, joined_ref, *refs):
         cosine_rows, sine_rows = cosine_ref[...], -sine_ref[...]
         for lane in range(0, model_width, LANES):
             block = slice(lane, lane + LANES)
@@ -378,85 +390,175 @@
             joined_ref[:, 2 * model_width + lane : 2 * model_width + lane + LANES] = (
                 grad_value.T.astype(BF16)
             )
-        write_weight_grad(h1_ref[...], joined_ref, refs[: len(outs)], refs[len(outs) :])
+        count = len(outs)
+        first, second = refs[:count], refs[count : 2 * count]
+        turned_context = refs[2 * count : 2 * count + len(scratch)]
+        turned, narrow = refs[2 * count + len(scratch) : -1], refs[-1]
+        narrow[...] = grad_middle_ref[...].astype(BF16)
+        write_weight_grad(context_ref[...], narrow, first, turned_context, 0)
+        write_weight_grad(
+            h1_ref[...], joined_ref.at[:, 2 * model_width :], first, turned, model_width
+        )
+        write_grad(turned[-1], joined_ref.at[:, : 2 * model_width], second, 0)
 
     results = run_kernel(
         body,
         "attention_backward",
-        [((slots, 3 * model_width), BF16)] + outs,
-        grad_scratch(model_width, slots),
-        [query, key, value, probs, context, grad_context, cosine, sine, h1],
-    )
-    return results[0], results[1:]
-
-
-def finish(tokens, middle, mixed, w_down_t, grad_joined, w_qkv, grad_middle, gains):
-    def body(tokens_ref, middle_ref, mixed_ref, w_down_ref, joined_ref, w_qkv_ref,
-             grad_middle_ref, gains_ref, output_ref, grad_ref):
+        [((slots, 3 * model_width), BF16)] + outs + outs,
+        scratch * 2 + [pltpu.VMEM((slots, model_width), BF16)],
+        [query, key, value, probs, context, grad_context, cosine, sine, h1, grad_middle],
+        microseconds=6,
+    )
+    count = len(outs)
+    return results[0], results[1 : 1 + count], results[1 + count :]
+
+
+def layer_output(middle, mixed, w_down_t):
+    def body(middle_ref, mixed_ref, w_down_ref, output_ref):
         output = middle_ref[...] + dot_nt(mixed_ref[...], w_down_ref[...])
         output_ref[...] = output.astype(BF16)
+
+    outs = [(middle.shape, BF16)]
+    operands = [middle, mixed, w_down_t]
+    return run_kernel(body, "layer_output", outs, [], operands, microseconds=2)[0]
+
+
+def input_grad(tokens, grad_joined, w_qkv, grad_middle, gains):
+    def body(tokens_ref, joined_ref, w_qkv_ref, grad_middle_ref, gains_ref, grad_ref):
         grad_h1 = dot_nt(joined_ref[...], w_qkv_ref[...])
         xhat, scale = normalised(tokens_ref[...].astype(F32))
         grad_ref[...] = grad_middle_ref[...] + norm_back(grad_h1, xhat, scale, gains_ref[0:1, :])
 
-    return run_kernel(
-        body,
-        "finish",
-        [(tokens.shape, BF16), (tokens.shape, F32)],
-        [],
-        [tokens, middle, mixed, w_down_t, grad_joined, w_qkv, grad_middle, gains],
-    )
+    outs = [(tokens.shape, F32)]
+    operands = [tokens, grad_joined, w_qkv, grad_middle, gains]
+    return run_kernel(body, "input_grad", outs, [], operands, microseconds=3)[0]
 
 
 def add(*parts):
-    return sum(part.astype(F32) for part in parts).astype(BF16)
-
-
-def scatter_sum(parts):
-    if len(parts) == 1:
-        return lax.psum_scatter(parts[0], "fsdp", scatter_dimension=0, tiled=True).astype(F32)
-    keep, send = parts
-    half = keep.shape[0] // 8
-    other = swap(send, CORE)
-
-    def chip(first, count):
-        rows = slice(first * half, (first + count) * half)
-        return add(keep[rows], other[rows])
-
-    by_x = swap(chip(0, 2), ALONG_X)
-    by_y = swap(chip(2, 2), ALONG_Y)
-    late_x = swap(add(keep[4 * half : 5 * half], other[4 * half : 5 * half], by_y[:half]), ALONG_X)
-    late_y = swap(add(keep[5 * half : 6 * half], other[5 * half : 6 * half], by_x[:half]), ALONG_Y)
-    own = keep[6 * half :].astype(F32) + other[6 * half :].astype(F32)
-    own += jnp.concatenate([by_x[half:], by_y[half:]], 0).astype(F32)
-    own += jnp.concatenate([late_y, late_x], 0).astype(F32)
-    return own
-
-
-def copies_sum(values):
-    copies = lax.axis_size("replica")
-    me = lax.axis_index("replica")
-    rows, width = values.shape
-    part = rows // copies
-    narrow = values.astype(BF16)
-
-    def shift(array, by):
-        return lax.ppermute(array, "replica", [(i, (i + by) % copies) for i in range(copies)])
-
-    def part_of(array, at):
-        return lax.dynamic_slice_in_dim(array, at * part, part, 0)
-
-    total = part_of(values, me)
-    for by in range(1, copies):
-        total += shift(part_of(narrow, (me + by) % copies), by).astype(F32)
-    total = total.astype(BF16)
-    result = jnp.zeros((copies, part, width), BF16)
-    result = lax.dynamic_update_index_in_dim(result, total, me, 0)
-    for by in range(1, copies):
-        result = lax.dynamic_update_index_in_dim(
-            result, shift(total, by), (me + copies - by) % copies, 0
-        )
-    return result.reshape(rows, width).astype(F32)
+    return sum(part.astype(F32) for part in parts)
+
+
+class Steps:
+    def hold(self, earlier, *names):
+        for name, held in zip(names, after([getattr(self, n) for n in names], *earlier)):
+            setattr(self, name, held)
+
+
+class ShardSum(Steps):
+    def __init__(self, parts):
+        self.keep, send = parts
+        self.half = self.keep.shape[0] // 8
+        self.other = swap(send, CORE)
+
+    def chip(self, first, count, *more):
+        rows = slice(first * self.half, (first + count) * self.half)
+        return add(self.keep[rows], self.other[rows], *more)
+
+    def ready_one(self):
+        self.to_x = self.chip(0, 2).astype(BF16)
+        self.to_y = self.chip(2, 2).astype(BF16)
+        return self.to_x, self.to_y
+
+    def send_one(self):
+        self.by_x, self.by_y = swap(self.to_x, ALONG_X), swap(self.to_y, ALONG_Y)
+
+    def ready_two(self):
+        self.late_x = self.chip(4, 1, self.by_y[: self.half]).astype(BF16)
+        self.late_y = self.chip(5, 1, self.by_x[: self.half]).astype(BF16)
+        return self.late_x, self.late_y
+
+    def send_two(self):
+        self.from_x, self.from_y = swap(self.late_x, ALONG_X), swap(self.late_y, ALONG_Y)
+
+    def result(self):
+        first = self.chip(6, 1, self.by_x[self.half :], self.from_y)
+        second = self.chip(7, 1, self.by_y[self.half :], self.from_x)
+        return first, second
+
+
+class CopiesSum(Steps):
+    def __init__(self, first, second):
+        self.odd = lax.axis_index("replica") % 2 == 1
+        self.mine = jnp.where(self.odd, second, first)
+        self.theirs = jnp.where(self.odd, first, second).astype(BF16)
+
+    def swap(self, values, mask):
+        return lax.ppermute(values, "replica", [(i, i ^ mask) for i in range(4)])
+
+    def send_one(self):
+        self.near = self.swap(self.theirs, 1)
+
+    def ready_two(self):
+        self.pair = add(self.mine, self.near).astype(BF16)
+        return self.pair
+
+    def send_two(self):
+        self.far = self.swap(self.pair, 2)
+
+    def send_three(self):
+        self.total = add(self.pair, self.far).astype(BF16)
+        self.back = self.swap(self.total, 1)
+
+
+def place_halves(total_ref, back_ref, out_ref, columns=slice(None)):
+    half = total_ref.shape[0]
+    odd = lax.rem(lax.axis_index("replica"), 2)
+    for ref, at in ((total_ref, odd), (back_ref, 1 - odd)):
+        rows = pl.ds(pl.multiple_of(at * half, half), half)
+        out_ref[rows, :] = ref[:, columns].astype(F32)
+
+
+def write_gain_grad(weight, weight_sum, gain_ref, out_ref):
+    column = jnp.sum(weight.astype(F32) * weight_sum, 1, keepdims=True)
+    row = jnp.broadcast_to(column, (column.shape[0], LANES)).T[:1]
+    out_ref[...] = row / gain_ref[...].astype(F32)
+
+
+def down_result(group):
+    half, width = group.total.shape
+
+    def body(total_ref, back_ref, out_ref):
+        place_halves(total_ref, back_ref, out_ref)
+
+    outs = [((2 * half, width), F32)]
+    return run_kernel(body, "down_result", outs, [], [group.total, group.back], microseconds=1)[0]
+
+
+def in_result(group, weight, gain):
+    half, width = group.total.shape
+
+    def body(total_ref, back_ref, weight_ref, gain_ref, out_ref, gain_out_ref):
+        place_halves(total_ref, back_ref, out_ref)
+        write_gain_grad(weight_ref[...], out_ref[...], gain_ref, gain_out_ref)
+
+    outs = [((2 * half, width), F32), ((1, 2 * half), F32)]
+    operands = [group.total, group.back, weight, gain[None]]
+    result, gain_result = run_kernel(body, "in_result", outs, [], operands, microseconds=1)
+    return result, gain_result[0]
+
+
+def attention_result(early, late, weight, gain):
+    half, width = early.total.shape
+    each = width // 2
+
+    def body(early_total, early_back, late_total, late_back, weight_ref, gain_ref,
+             qkv_ref, out_ref, gain_out_ref):
+        place_halves(late_total, late_back, qkv_ref.at[:, :width])
+        place_halves(early_total, early_back, qkv_ref.at[:, width:], slice(each, width))
+        place_halves(early_total, early_back, out_ref, slice(0, each))
+        write_gain_grad(weight_ref[...], qkv_ref[...], gain_ref, gain_out_ref)
+
+    outs = [((2 * half, 3 * each), F32), ((2 * half, each), F32), ((1, 2 * half), F32)]
+    operands = [early.total, early.back, late.total, late.back, weight, gain[None]]
+    qkv, out, gain_result = run_kernel(
+        body, "attention_result", outs, [], operands, microseconds=1
+    )
+    return qkv, out, gain_result[0]
+
+
+def whole_sum(part):
+    shard = lax.psum_scatter(part, "fsdp", scatter_dimension=0, tiled=True)
+    return lax.psum(shard, "replica").astype(F32)
 
 
 def per_device(
@@ -474,8 +576,17 @@
     qkv_width, out_width = qkv_weight.shape[1], out_weight.shape[1]
     in_width, ff_width = in_weight.shape[1], down_weight.shape[0]
     gain_columns = jnp.pad(jnp.stack([norm1_gain, norm2_gain], 1), ((0, 0), (0, LANES - 2)))
-    attn_pieces = gathered(jnp.concatenate([qkv_weight, out_weight, gain_columns], 1))
-    mlp_pieces = gathered(jnp.concatenate([in_weight, down_weight.T], 1))
+    attn_own = jnp.concatenate([qkv_weight, out_weight, gain_columns], 1)
+    mlp_own = jnp.concatenate([in_weight, down_weight.T], 1)
+    exchange = lax.axis_size("fsdp") == 8 and lax.axis_size("replica") == 4
+    if exchange:
+        attn_first = gather_first(attn_own)
+        attn_second = gather_second(*attn_first[:3])
+        attn_pieces = gather_third(attn_first, attn_second)
+        mlp_own = after(mlp_own, *attn_second)
+        mlp_first = gather_first(mlp_own)
+    else:
+        attn_pieces, mlp_pieces = gathered_whole(attn_own), gathered_whole(mlp_own)
     positions = slot_layout(seq_lengths, slot_count)[1][0]
     cosine, sine = rope_tables(positions, HEAD)
     cosine = jnp.concatenate([cosine] * 4, 1)
@@ -484,39 +595,96 @@
     (h1, query, key, value, probs, context, middle, h2, w_qkv, w_out, gains) = attention_forward(
         seq_lengths, tokens, cosine, sine, attn_pieces, qkv_width, out_width
     )
+    if exchange:
+        mlp_first = after(mlp_first, h2)
+        mlp_pieces = gather_third(mlp_first, gather_second(*mlp_first[:3]))
     (mixed, grad_hidden, w_in, w_down_t), down_parts = feed_forward(
         h2, cotangent, mlp_pieces, in_width, ff_width
     )
-    down_shard = scatter_sum(down_parts)
-    in_shard = scatter_sum(weight_grad(h2, grad_hidden))
-    (grad_middle, grad_context), out_parts = middle_backward(
-        grad_hidden, w_in, middle, gains, cotangent, w_out, context
-    )
-    out_shard = scatter_sum(out_parts)
-    grad_joined, qkv_parts = attention_backward(
-        query, key, value, probs, context, grad_context, cosine, sine, h1
-    )
-    qkv_shard = scatter_sum(qkv_parts)
-    output, grad_tokens = finish(
-        tokens, middle, mixed, w_down_t, grad_joined, w_qkv, grad_middle, gains
-    )
-    mlp_sum = copies_sum(jnp.concatenate([in_shard, down_shard], 1))
-    attn_sum = copies_sum(jnp.concatenate([qkv_shard, out_shard], 1))
-    grad_qkv, grad_out = attn_sum[:, :qkv_width], attn_sum[:, qkv_width:]
-    grad_in, grad_down = mlp_sum[:, :in_width], mlp_sum[:, in_width:].T
-
-    def gain_grad(weight, weight_sum, gain):
-        return jnp.sum(weight.astype(F32) * weight_sum, 1) / gain.astype(F32)
+    if exchange:
+        down = ShardSum(down_parts)
+    in_parts = weight_grad(h2, grad_hidden)
+    if exchange:
+        into = ShardSum(in_parts)
+        down.hold(in_parts, "other")
+        grad_hidden = after(grad_hidden, *down.ready_one())
+        down.send_one()
+    grad_middle, grad_context = middle_backward(
+        grad_hidden, w_in, middle, gains, cotangent, w_out
+    )
+    if exchange:
+        into.hold([grad_context], "other")
+        down.hold([grad_context], "by_x", "by_y")
+        grad_context = after(grad_context, *into.ready_one(), *down.ready_two())
+        into.send_one()
+        down.send_two()
+    grad_joined, early_parts, late_parts = attention_backward(
+        query, key, value, probs, context, grad_context, cosine, sine, h1, grad_middle
+    )
+    if exchange:
+        early, late = ShardSum(early_parts), ShardSum(late_parts)
+        down.hold([grad_joined], "from_x", "from_y")
+        down_copies = CopiesSum(*down.result())
+        mixed = after(mixed, *early.ready_one(), down_copies.theirs)
+        down_copies.send_one()
+        early.send_one()
+    output = layer_output(middle, mixed, w_down_t)
+    if exchange:
+        into.hold([output], "by_x", "by_y")
+        down_copies.hold([output], "near")
+        late.hold([output], "other")
+        grad_middle = after(grad_middle, *into.ready_two(), *late.ready_one(), down_copies.ready_two())
+        into.send_two()
+        late.send_one()
+        down_copies.send_two()
+    grad_tokens = input_grad(tokens, grad_joined, w_qkv, grad_middle, gains)
+    if exchange:
+        early.hold([grad_tokens], "by_x", "by_y")
+        into.hold([grad_tokens], "from_x", "from_y")
+        late.hold([grad_tokens], "by_x", "by_y")
+        early.ready_two()
+        early.send_two()
+        into_copies = CopiesSum(*into.result())
+        into_copies.send_one()
+        late.ready_two()
+        late.send_two()
+        down_copies.send_three()
+        into_copies.ready_two()
+        into_copies.send_two()
+        into_copies.send_three()
+        early_copies = CopiesSum(*early.result())
+        late_copies = CopiesSum(*late.result())
+        for group in (early_copies, late_copies):
+            group.send_one()
+            group.ready_two()
+            group.send_two()
+            group.send_three()
+        grad_down = down_result(down_copies)
+        grad_in, grad_norm2 = in_result(into_copies, in_weight, norm2_gain)
+        grad_qkv, grad_out, grad_norm1 = attention_result(
+            early_copies, late_copies, qkv_weight, norm1_gain
+        )
+    else:
+        grad_down, grad_in = whole_sum(down_parts[0]), whole_sum(in_parts[0])
+        early_sum, late_sum = whole_sum(early_parts[0]), whole_sum(late_parts[0])
+        grad_out, grad_values = early_sum[:, :out_width], early_sum[:, out_width:]
+        grad_qkv = jnp.concatenate([late_sum, grad_values], 1)
+
+        def gain_grad(weight, weight_sum, gain):
+            return jnp.sum(weight.astype(F32) * weight_sum, 1) / gain.astype(F32)
+
+        grad_norm1 = gain_grad(qkv_weight, grad_qkv, norm1_gain)
+        grad_norm2 = gain_grad(in_weight, grad_in, norm2_gain)
 
     return (
         output,
         grad_tokens,
-        gain_grad(qkv_weight, grad_qkv, norm1_gain),
+        grad_norm1,
         grad_qkv,
         grad_out,
-        gain_grad(in_weight, grad_in, norm2_gain),
+        grad_norm2,
         grad_in,
-        grad_down,
+        grad_down.T,
     )
 
 

time: 211 us -> 165 us (0.78)
  starting transfers between devices: 64 us -> 45.7 us
  Pallas kernels: 37.3 us -> 26.7 us
  local copies, waits for them, and re-layouts: 16.7 us -> 7.22 us
  waiting for transfers between devices: 72 us -> 67.6 us
  other arithmetic: 17.5 us -> 14.8 us
    ppermute x12, starting transfers between devices: 34.5 us -> 14.2 us  [swap(): return lax.ppermute(values, 'replica', [(i, i ^ mask) for i in range(4)])]
    ppermute x38, waiting for transfers between devices: 61.2 us -> 49 us  [swap(): return lax.ppermute(values, 'fsdp', [(i, i ^ mask) for i in range(8)])]
    pallas_call x6 -> x10, Pallas kernels: 37.3 us -> 26.7 us  [run_kernel(): pl.pallas_call(body, out_shape=[jax.ShapeDtypeStruct(shape, kind) for sha...]
    ppermute x12, waiting for transfers between devices: 10.8 us -> 18.6 us  [swap(): return lax.ppermute(values, 'replica', [(i, i ^ mask) for i in range(4)])]
    unnamed x80 -> x64, local copies, waits for them, and re-layouts: 13.9 us -> 6.42 us
    convert_element_type x12 -> x20, other arithmetic: 7.62 us -> 11.5 us  [the longest x4 3.34 us: ready_two(): self.pair = add(self.mine, self.near).astype(BF16)]
    add x4 -> x0, other arithmetic: 3.66 us -> none  [scatter_sum(): own += jnp.concatenate([late_y, late_x], 0).astype(F32)]
    reduce_sum x2 -> x0, other arithmetic: 2.2 us -> none  [gain_grad(): return jnp.sum(weight.astype(F32) * weight_sum, 1) / gain.astype(F32)]
  transfers between devices with their start and end apart: 50 -> 50, of which waited for: 18 -> 28; matrix products, arithmetic and copies ran while one was open for 8% -> 8% of each run, Pallas kernels for 14% -> 10%
where the time goes in v3:
time: 165 us; the launch traced here: 164 us
  waiting for transfers between devices  67.6 us (41%)
  starting transfers between devices  45.7 us (28%)
  Pallas kernels  26.7 us (16%)
  other arithmetic  14.8 us (9%)
  local copies, waits for them, and re-layouts  7.22 us (4%)
  between operations  2.34 us (1%)
    ppermute x38, waiting for transfers between devices, swap(): return lax.ppermute(values, 'fsdp', [(i, i ^ mask) for i in range(8)])  49 us
    ppermute x38, starting transfers between devices, swap(): return lax.ppermute(values, 'fsdp', [(i, i ^ mask) for i in range(8)])  31.4 us
    pallas_call x10, Pallas kernels, run_kernel(): pl.pallas_call(body, out_shape=[jax.ShapeDtypeStruct(shape, kind) for sha...  26.7 us
    ppermute x12, waiting for transfers between devices, swap(): return lax.ppermute(values, 'replica', [(i, i ^ mask) for i in range(4)])  18.6 us
    ppermute x12, starting transfers between devices, swap(): return lax.ppermute(values, 'replica', [(i, i ^ mask) for i in range(4)])  14.2 us
    unnamed x64, local copies, waits for them, and re-layouts  6.42 us
    convert_element_type x4, other arithmetic, ready_two(): self.pair = add(self.mine, self.near).astype(BF16)  3.34 us
  transfers between devices with their start and end apart: 50, of which 28 were waited for; matrix products, arithmetic and copies ran while one was open for 8% of the time, Pallas kernels for 10%

profile of v3, /device:TPU:0, one launch (start us, length us, event | category | flops | bytes accessed | tf_op | source)
XLA Modules:
  0.0 164.3 jit_solution(11464947464967470912)
XLA Ops:
  2.6 3.0 %collective-permute-start.1 = (bf16[96,3200]{1,0:T(8,128)(2,1)S(1)}, bf16[96,3200]{1,0:T(8,128)(2,1)S(1)}, u32[]{:S(2)}, u32[]{:S(2)}) collective-permute-start(bf16[96,3200]{1,0:T(8,128)(2,1)S(1)} %fusion.1.refs_4_), channel_id=1, source_target_pairs={{0,4},{1,5},{2,6},{3,7},{4,0},{5,1},{6,2},{7,3},{8,12},{9,13},{10,... | collective-permute-start | bytes 1843208 | tf_op jit(solution)/shard_map/ppermute | solution.py:58
  9.7 9.8 %collective-permute-done.1.refs_6_ = bf16[96,3200]{1,0:T(8,128)(2,1)S(1)} collective-permute-done((bf16[96,3200]{1,0:T(8,128)(2,1)S(1)}, bf16[96,3200]{1,0:T(8,128)(2,1)S(1)}, u32[]{:S(2)}, u32[]{:S(2)}) %collective-permute-start.1) | collective-permute-done | bytes 614432 | tf_op jit(solution)/shard_map/ppermute | solution.py:58
  19.5 1.8 %collective-permute-start.2 = (bf16[48,3200]{1,0:T(8,128)(2,1)S(1)}, bf16[48,3200]{1,0:T(8,128)(2,1)S(1)}, u32[]{:S(2)}, u32[]{:S(2)}) collective-permute-start(bf16[48,3200]{1,0:T(8,128)(2,1)S(1)} %slice.280), channel_id=1, source_target_pairs={{0,2},{1,3},{2,0},{3,1},{4,6},{5,7},{6,4},{7,5},{8,10},{9,11},{10,... | collective-permute-start | bytes 921608 | tf_op jit(solution)/shard_map/ppermute | solution.py:58
  24.3 3.8 %collective-permute-done.2.refs_7_ = bf16[48,3200]{1,0:T(8,128)(2,1)S(1)} collective-permute-done((bf16[48,3200]{1,0:T(8,128)(2,1)S(1)}, bf16[48,3200]{1,0:T(8,128)(2,1)S(1)}, u32[]{:S(2)}, u32[]{:S(2)}) %collective-permute-start.2) | collective-permute-done | bytes 307232 | tf_op jit(solution)/shard_map/ppermute | solution.py:58
  32.0 7.3 %attention_forward.1 = (bf16[256,768]{1,0:T(8,128)(2,1)S(1)}, bf16[256,768]{1,0:T(8,128)(2,1)S(1)}, bf16[256,768]{1,0:T(8,128)(2,1)S(1)}, bf16[256,768]{1,0:T(8,...) custom-call(s32[1,2]{1,0:T(1,128)S(1)} %copy-done.5, ...), custom_call_target="tpu_custom_call" | custom-call | flops 11000000512 | tf_op jit(solution)/shard_map/attention_forward/pallas_call | solution.py:43
  39.3 1.8 %copy-done.12 = bf16[768,2304]{1,0:T(8,128)(2,1)} copy-done((bf16[768,2304]{1,0:T(8,128)(2,1)}, bf16[768,2304]{1,0:T(8,128)(2,1)S(1)}, u32[]{:S(2)}) %copy-start.12) | copy-done | bytes 3538968
  41.1 5.7 %collective-permute-done.10.refs_4_ = bf16[96,3456]{1,0:T(8,128)(2,1)S(1)} collective-permute-done((bf16[96,3456]{1,0:T(8,128)(2,1)S(1)}, bf16[96,3456]{1,0:T(8,128)(2,1)S(1)}, u32[]{:S(2)}, u32[]{:S(2)}) %collective-permute-start.10) | collective-permute-done | bytes 663584 | tf_op jit(solution)/shard_map/ppermute | solution.py:58
  50.7 6.9 %collective-permute-done.12.refs_5_ = bf16[48,3456]{1,0:T(8,128)(2,1)S(1)} collective-permute-done((bf16[48,3456]{1,0:T(8,128)(2,1)S(1)}, bf16[48,3456]{1,0:T(8,128)(2,1)S(1)}, u32[]{:S(2)}, u32[]{:S(2)}) %collective-permute-start.12) | collective-permute-done | bytes 331808 | tf_op jit(solution)/shard_map/ppermute | solution.py:58
  59.7 4.0 %feed_forward.1 = (bf16[256,1152]{1,0:T(8,128)(2,1)S(1)}, bf16[256,2304]{1,0:T(8,128)(2,1)S(1)}, bf16[768,2304]{1,0:T(8,128)(2,1)S(1)}, bf16[768,1152]{1,0:T(8,1...) custom-call(bf16[256,768]{1,0:T(8,128)(2,1)S(1)} %get-tuple-element.65.refs_0_.rows_ref, ...), custom_call_target="tpu_custom_call" | custom-call | flops 8000000000 | tf_op jit(solution)/shard_map/feed_forward/pallas_call | solution.py:43
  63.9 1.7 %weight_grad.1 = (bf16[384,2304]{1,0:T(8,128)(2,1)S(1)}, bf16[384,2304]{1,0:T(8,128)(2,1)S(1)}) custom-call(bf16[256,768]{1,0:T(8,128)(2,1)S(1)} %get-tuple-element.65.refs_0_.rows_ref, bf16[256,2304]{1,0:T(8,128)(2,1)S(1)} %get-tuple-element.83.columns_ref.grad_hidden_ref), custom_call_target="tpu_custom_call" | custom-call | flops 1500000000 | tf_op jit(solution)/shard_map/weight_grad/pallas_call | solution.py:43
  68.6 2.3 %middle_backward.1 = (f32[256,768]{1,0:T(8,128)S(1)}, bf16[256,768]{1,0:T(8,128)(2,1)S(1)}) custom-call(bf16[256,2304]{1,0:T(8,128)(2,1)S(1)} %get-tuple-element.83.columns_ref.grad_hidden_ref, bf16[768,2304]{1,0:T(8,128)(2,1)S(1)} %get-tuple-element.84.w_in_ref, f32[256,768]{1,0:T(8,128)S(1)} %get-tuple-element.64.middle_ref, ...), custom_call_target="tpu_custom_call" | custom-call | flops 5000000000 | tf_op jit(solution)/shard_map/middle_backward/pallas_call | solution.py:43
  70.9 2.9 %collective-permute-done.20 = bf16[96,1152]{1,0:T(8,128)(2,1)S(1)} collective-permute-done((bf16[96,1152]{1,0:T(8,128)(2,1)S(1)}, bf16[96,1152]{1,0:T(8,128)(2,1)S(1)}, u32[]{:S(2)}, u32[]{:S(2)}) %collective-permute-start.20) | collective-permute-done | bytes 221216 | tf_op jit(solution)/shard_map/ppermute | solution.py:58
  77.3 4.6 %attention_backward.1 = (bf16[256,2304]{1,0:T(8,128)(2,1)S(1)}, bf16[384,1536]{1,0:T(8,128)(2,1)S(1)}, bf16[384,1536]{1,0:T(8,128)(2,1)}, bf16[384,1536]{1,0:T(8,128)(2,1)S(1)}, bf16[384,1536]{1,0:T(8,128)(2,1)S(1)}) custom-call(bf16[256,768]{1,0:T(8,128)(2,1)S(1)} %get-tuple-element.72.q_ref, bf16[256,768]{1,0:T(8,128)(2,1)S(1)} %get-tuple-element.73.k_ref, ...), custom_call_target="tpu_custom_call" | custom-call | flops 6000000000 | tf_op jit(solution)/shard_map/attention_backward/pallas_call | solution.py:43
  89.2 2.0 %collective-permute-done.23 = bf16[48,1152]{1,0:T(8,128)(2,1)S(1)} collective-permute-done((bf16[48,1152]{1,0:T(8,128)(2,1)}, bf16[48,1152]{1,0:T(8,128)(2,1)S(1)}, u32[]{:S(2)}, u32[]{:S(2)}) %collective-permute-start.23) | collective-permute-done | bytes 110624 | tf_op jit(solution)/shard_map/ppermute | solution.py:58
  100.6 2.7 %collective-permute-start.48 = (bf16[48,1152]{1,0:T(8,128)(2,1)S(1)}, bf16[48,1152]{1,0:T(8,128)(2,1)S(1)}, u32[]{:S(2)}, u32[]{:S(2)}) collective-permute-start(bf16[48,1152]{1,0:T(8,128)(2,1)S(1)} %add_convert_fusion.21), channel_id=1, source_target_pairs={{0,16},{8,24},{16,0},{24,8},{1,17},{9,25},{17,1},{25,9},{2,18},{10... | collective-permute-start | bytes 331784 | tf_op jit(solution)/shard_map/ppermute | solution.py:486
  107.8 2.3 %input_grad.1 = f32[256,768]{1,0:T(8,128)} custom-call(bf16[256,768]{1,0:T(8,128)(2,1)S(1)} %copy-done.9, bf16[256,2304]{1,0:T(8,128)(2,1)S(1)} %copy-done.17, bf16[768,2304]{1,0:T(8,128)(2,1)S(1)} %copy-done.13, f32[256,768]{1,0:T(8,128)S(1)} %copy-done.21, f32[8,768]{1,0:T(8,128)S(1)} %get-tuple-element.85.gains_ref), custom_call_target="tpu_custom_call" | custom-call | flops 3000000000 | tf_op jit(solution)/shard_map/input_grad/pallas_call | solution.py:43
  114.6 3.6 %collective-permute-done.36 = bf16[96,1536]{1,0:T(8,128)(2,1)S(1)} collective-permute-done((bf16[96,1536]{1,0:T(8,128)(2,1)S(1)}, bf16[96,1536]{1,0:T(8,128)(2,1)S(1)}, u32[]{:S(2)}, u32[]{:S(2)}) %collective-permute-start.36) | collective-permute-done | bytes 294944 | tf_op jit(solution)/shard_map/ppermute | solution.py:58
  120.9 3.6 %collective-permute-done.29 = bf16[96,1536]{1,0:T(8,128)(2,1)S(1)} collective-permute-done((bf16[96,1536]{1,0:T(8,128)(2,1)S(1)}, bf16[96,1536]{1,0:T(8,128)(2,1)S(1)}, u32[]{:S(2)}, u32[]{:S(2)}) %collective-permute-start.29) | collective-permute-done | bytes 294944 | tf_op jit(solution)/shard_map/ppermute | solution.py:58
  126.3 1.7 %collective-permute-start.31 = (bf16[48,1536]{1,0:T(8,128)(2,1)S(1)}, bf16[48,1536]{1,0:T(8,128)(2,1)S(1)}, u32[]{:S(2)}, u32[]{:S(2)}) collective-permute-start(bf16[48,1536]{1,0:T(8,128)(2,1)S(1)} %get-tuple-element.127), channel_id=1, source_target_pairs={{0,2},{1,3},{2,0},{3,1},{4,6},{5,7},{6,4},{7,5},{8,10},{9,11},{10,... | collective-permute-start | bytes 442376 | tf_op jit(solution)/shard_map/ppermute | solution.py:58
  135.5 3.7 %collective-permute-done.40 = bf16[48,1536]{1,0:T(8,128)(2,1)S(1)} collective-permute-done((bf16[48,1536]{1,0:T(8,128)(2,1)S(1)}, bf16[48,1536]{1,0:T(8,128)(2,1)S(1)}, u32[]{:S(2)}, u32[]{:S(2)}) %collective-permute-start.40) | collective-permute-done | bytes 147488 | tf_op jit(solution)/shard_map/ppermute | solution.py:486
  139.4 2.9 %collective-permute-start.41 = (bf16[48,1536]{1,0:T(8,128)(2,1)S(1)}, bf16[48,1536]{1,0:T(8,128)(2,1)S(1)}, u32[]{:S(2)}, u32[]{:S(2)}) collective-permute-start(bf16[48,1536]{1,0:T(8,128)(2,1)S(1)} %add_convert_fusion.13), channel_id=1, source_target_pairs={{0,16},{8,24},{16,0},{24,8},{1,17},{9,25},{17,1},{25,9},{2,18},{10... | collective-permute-start | bytes 442376 | tf_op jit(solution)/shard_map/ppermute | solution.py:486
  144.9 6.1 %collective-permute-done.41 = bf16[48,1536]{1,0:T(8,128)(2,1)S(1)} collective-permute-done((bf16[48,1536]{1,0:T(8,128)(2,1)S(1)}, bf16[48,1536]{1,0:T(8,128)(2,1)S(1)}, u32[]{:S(2)}, u32[]{:S(2)}) %collective-permute-start.41) | collective-permute-done | bytes 147488 | tf_op jit(solution)/shard_map/ppermute | solution.py:486
  155.6 2.1 %collective-permute-done.42.late_back = bf16[48,1536]{1,0:T(8,128)(2,1)S(1)} collective-permute-done((bf16[48,1536]{1,0:T(8,128)(2,1)S(1)}, bf16[48,1536]{1,0:T(8,128)(2,1)S(1)}, u32[]{:S(2)}, u32[]{:S(2)}) %collective-permute-start.42) | collective-permute-done | bytes 147488 | tf_op jit(solution)/shard_map/ppermute | solution.py:486
  157.8 3.1 %collective-permute-done.35.early_back = bf16[48,1536]{1,0:T(8,128)(2,1)S(1)} collective-permute-done((bf16[48,1536]{1,0:T(8,128)(2,1)S(1)}, bf16[48,1536]{1,0:T(8,128)(2,1)S(1)}, u32[]{:S(2)}, u32[]{:S(2)}) %collective-permute-start.35) | collective-permute-done | bytes 147488 | tf_op jit(solution)/shard_map/ppermute | solution.py:486
  (183 shorter events, 72.7 us)
Async XLA Ops:
  2.6 16.9 %collective-permute-start.1 = (bf16[96,3200]{1,0:T(8,128)(2,1)S(1)}, bf16[96,3200]{1,0:T(8,128)(2,1)S(1)}, u32[]{:S(2)}, u32[]{:S(2)}) collective-permute-start(bf16[96,3200]{1,0:T(8,128)(2,1)S(1)} %fusion.1.refs_4_), channel_id=1, source_target_pairs={{0,4},{1,5},{2,6},{3,7},{4,0},{5,1},{6,2},{7,3},{8,12},{9,13},{10,... | collective-permute-start | bytes 1843208 | tf_op jit(solution)/shard_map/ppermute | solution.py:58
  5.7 15.7 %collective-permute-start = (bf16[96,3200]{1,0:T(8,128)(2,1)S(1)}, bf16[96,3200]{1,0:T(8,128)(2,1)S(1)}, u32[]{:S(2)}, u32[]{:S(2)}) collective-permute-start(bf16[96,3200]{1,0:T(8,128)(2,1)S(1)} %fusion.1.refs_4_), channel_id=1, source_target_pairs={{0,2},{1,3},{2,0},{3,1},{4,6},{5,7},{6,4},{7,5},{8,10},{9,11},{10,... | collective-permute-start | bytes 1843208 | tf_op jit(solution)/shard_map/ppermute | solution.py:58
  7.1 22.2 %collective-permute-start.4 = (bf16[96,3200]{1,0:T(8,128)(2,1)S(1)}, bf16[96,3200]{1,0:T(8,128)(2,1)S(1)}, u32[]{:S(2)}, u32[]{:S(2)}) collective-permute-start(bf16[96,3200]{1,0:T(8,128)(2,1)S(1)} %fusion.1.refs_4_), channel_id=1, source_target_pairs={{0,1},{1,0},{2,3},{3,2},{4,5},{5,4},{6,7},{7,6},{8,9},{9,8},{10,11... | collective-permute-start | bytes 1843208 | tf_op jit(solution)/shard_map/ppermute | solution.py:58
  29.4 17.4 %collective-permute-start.10 = (bf16[96,3456]{1,0:T(8,128)(2,1)S(1)}, bf16[96,3456]{1,0:T(8,128)(2,1)S(1)}, u32[]{:S(2)}, u32[]{:S(2)}) collective-permute-start(bf16[96,3456]{1,0:T(8,128)(2,1)S(1)} %pad_maximum_fusion.refs_2_), channel_id=1, source_target_pairs={{0,4},{1,5},{2,6},{3,7},{4,0},{5,1},{6,2},{7,3},{8,12},{9,13},{10,... | collective-permute-start | bytes 1990664 | tf_op jit(solution)/shard_map/ppermute | solution.py:58
  30.9 15.8 %collective-permute-start.11 = (bf16[96,3456]{1,0:T(8,128)(2,1)S(1)}, bf16[96,3456]{1,0:T(8,128)(2,1)S(1)}, u32[]{:S(2)}, u32[]{:S(2)}) collective-permute-start(bf16[96,3456]{1,0:T(8,128)(2,1)S(1)} %pad_maximum_fusion.refs_2_), channel_id=1, source_target_pairs={{0,1},{1,0},{2,3},{3,2},{4,5},{5,4},{6,7},{7,6},{8,9},{9,8},{10,11... | collective-permute-start | bytes 1990664 | tf_op jit(solution)/shard_map/ppermute | solution.py:58
  31.2 17.1 %collective-permute-start.9 = (bf16[96,3456]{1,0:T(8,128)(2,1)S(1)}, bf16[96,3456]{1,0:T(8,128)(2,1)S(1)}, u32[]{:S(2)}, u32[]{:S(2)}) collective-permute-start(bf16[96,3456]{1,0:T(8,128)(2,1)S(1)} %pad_maximum_fusion.refs_2_), channel_id=1, source_target_pairs={{0,2},{1,3},{2,0},{3,1},{4,6},{5,7},{6,4},{7,5},{8,10},{9,11},{10,... | collective-permute-start | bytes 1990664 | tf_op jit(solution)/shard_map/ppermute | solution.py:58
  50.1 9.5 %collective-permute-start.14 = (bf16[96,3456]{1,0:T(8,128)(2,1)S(1)}, bf16[96,3456]{1,0:T(8,128)(2,1)S(1)}, u32[]{:S(2)}, u32[]{:S(2)}) collective-permute-start(bf16[96,3456]{1,0:T(8,128)(2,1)S(1)} %collective-permute-done.9.refs_3_), channel_id=1, source_target_pairs={{0,1},{1,0},{2,3},{3,2},{4,5},{5,4},{6,7},{7,6},{8,9},{9,8},{10,11... | collective-permute-start | bytes 1990664 | tf_op jit(solution)/shard_map/ppermute | solution.py:58
  50.2 9.5 %collective-permute-start.15 = (bf16[96,3456]{1,0:T(8,128)(2,1)S(1)}, bf16[96,3456]{1,0:T(8,128)(2,1)S(1)}, u32[]{:S(2)}, u32[]{:S(2)}) collective-permute-start(bf16[96,3456]{1,0:T(8,128)(2,1)S(1)} %collective-permute-done.10.refs_4_), channel_id=1, source_target_pairs={{0,1},{1,0},{2,3},{3,2},{4,5},{5,4},{6,7},{7,6},{8,9},{9,8},{10,11... | collective-permute-start | bytes 1990664 | tf_op jit(solution)/shard_map/ppermute | solution.py:58
  65.7 10.1 %collective-permute-start.19 = (bf16[384,2304]{1,0:T(8,128)(2,1)S(1)}, bf16[384,2304]{1,0:T(8,128)(2,1)S(1)}, u32[]{:S(2)}, u32[]{:S(2)}) collective-permute-start(bf16[384,2304]{1,0:T(8,128)(2,1)S(1)} %get-tuple-element.81), channel_id=1, source_target_pairs={{0,1},{1,0},{2,3},{3,2},{4,5},{5,4},{6,7},{7,6},{8,9},{9,8},{10,11... | collective-permute-start | bytes 5308424 | tf_op jit(solution)/shard_map/ppermute | solution.py:58
  85.1 10.0 %collective-permute-start.22 = (bf16[384,1536]{1,0:T(8,128)(2,1)}, bf16[384,1536]{1,0:T(8,128)(2,1)}, u32[]{:S(2)}, u32[]{:S(2)}) collective-permute-start(bf16[384,1536]{1,0:T(8,128)(2,1)} %get-tuple-element.95), channel_id=1, source_target_pairs={{0,1},{1,0},{2,3},{3,2},{4,5},{5,4},{6,7},{7,6},{8,9},{9,8},{10,11... | collective-permute-start | bytes 3538952 | tf_op jit(solution)/shard_map/ppermute | solution.py:58
  86.7 16.6 %collective-permute-start.25 = (bf16[96,2304]{1,0:T(8,128)(2,1)}, bf16[96,2304]{1,0:T(8,128)(2,1)S(1)}, u32[]{:S(2)}, u32[]{:S(2)}) collective-permute-start(bf16[96,2304]{1,0:T(8,128)(2,1)} %get-tuple-element.123), channel_id=1, source_target_pairs={{0,2},{1,3},{2,0},{3,1},{4,6},{5,7},{6,4},{7,5},{8,10},{9,11},{10,... | collective-permute-start | bytes 1327112 | tf_op jit(solution)/shard_map/ppermute | solution.py:58
  88.0 15.2 %collective-permute-start.26 = (bf16[96,2304]{1,0:T(8,128)(2,1)}, bf16[96,2304]{1,0:T(8,128)(2,1)S(1)}, u32[]{:S(2)}, u32[]{:S(2)}) collective-permute-start(bf16[96,2304]{1,0:T(8,128)(2,1)} %get-tuple-element.122), channel_id=1, source_target_pairs={{0,4},{1,5},{2,6},{3,7},{4,0},{5,1},{6,2},{7,3},{8,12},{9,13},{10,... | collective-permute-start | bytes 1327112 | tf_op jit(solution)/shard_map/ppermute | solution.py:58
  91.9 11.3 %collective-permute-start.27 = (bf16[384,1536]{1,0:T(8,128)(2,1)}, bf16[384,1536]{1,0:T(8,128)(2,1)S(1)}, u32[]{:S(2)}, u32[]{:S(2)}) collective-permute-start(bf16[384,1536]{1,0:T(8,128)(2,1)} %copy-done.6), channel_id=1, source_target_pairs={{0,1},{1,0},{2,3},{3,2},{4,5},{5,4},{6,7},{7,6},{8,9},{9,8},{10,11... | collective-permute-start | bytes 3538952 | tf_op jit(solution)/shard_map/ppermute | solution.py:58
  100.6 9.5 %collective-permute-start.48 = (bf16[48,1152]{1,0:T(8,128)(2,1)S(1)}, bf16[48,1152]{1,0:T(8,128)(2,1)S(1)}, u32[]{:S(2)}, u32[]{:S(2)}) collective-permute-start(bf16[48,1152]{1,0:T(8,128)(2,1)S(1)} %add_convert_fusion.21), channel_id=1, source_target_pairs={{0,16},{8,24},{16,0},{24,8},{1,17},{9,25},{17,1},{25,9},{2,18},{10... | collective-permute-start | bytes 331784 | tf_op jit(solution)/shard_map/ppermute | solution.py:486
  106.0 12.2 %collective-permute-start.36 = (bf16[96,1536]{1,0:T(8,128)(2,1)S(1)}, bf16[96,1536]{1,0:T(8,128)(2,1)S(1)}, u32[]{:S(2)}, u32[]{:S(2)}) collective-permute-start(bf16[96,1536]{1,0:T(8,128)(2,1)S(1)} %get-tuple-element.129), channel_id=1, source_target_pairs={{0,2},{1,3},{2,0},{3,1},{4,6},{5,7},{6,4},{7,5},{8,10},{9,11},{10,... | collective-permute-start | bytes 884744 | tf_op jit(solution)/shard_map/ppermute | solution.py:58
  106.4 13.2 %collective-permute-start.37 = (bf16[96,1536]{1,0:T(8,128)(2,1)S(1)}, bf16[96,1536]{1,0:T(8,128)(2,1)S(1)}, u32[]{:S(2)}, u32[]{:S(2)}) collective-permute-start(bf16[96,1536]{1,0:T(8,128)(2,1)S(1)} %get-tuple-element.128), channel_id=1, source_target_pairs={{0,4},{1,5},{2,6},{3,7},{4,0},{5,1},{6,2},{7,3},{8,12},{9,13},{10,... | collective-permute-start | bytes 884744 | tf_op jit(solution)/shard_map/ppermute | solution.py:58
  110.1 14.4 %collective-permute-start.29 = (bf16[96,1536]{1,0:T(8,128)(2,1)S(1)}, bf16[96,1536]{1,0:T(8,128)(2,1)S(1)}, u32[]{:S(2)}, u32[]{:S(2)}) collective-permute-start(bf16[96,1536]{1,0:T(8,128)(2,1)S(1)} %get-tuple-element.131), channel_id=1, source_target_pairs={{0,2},{1,3},{2,0},{3,1},{4,6},{5,7},{6,4},{7,5},{8,10},{9,11},{10,... | collective-permute-start | bytes 884744 | tf_op jit(solution)/shard_map/ppermute | solution.py:58
  111.9 13.3 %collective-permute-start.30 = (bf16[96,1536]{1,0:T(8,128)(2,1)S(1)}, bf16[96,1536]{1,0:T(8,128)(2,1)S(1)}, u32[]{:S(2)}, u32[]{:S(2)}) collective-permute-start(bf16[96,1536]{1,0:T(8,128)(2,1)S(1)} %get-tuple-element.130), channel_id=1, source_target_pairs={{0,4},{1,5},{2,6},{3,7},{4,0},{5,1},{6,2},{7,3},{8,12},{9,13},{10,... | collective-permute-start | bytes 884744 | tf_op jit(solution)/shard_map/ppermute | solution.py:58
  113.3 41.5 %collective-permute-start.49 = (bf16[48,1152]{1,0:T(8,128)(2,1)S(1)}, bf16[48,1152]{1,0:T(8,128)(2,1)S(1)}, u32[]{:S(2)}, u32[]{:S(2)}) collective-permute-start(bf16[48,1152]{1,0:T(8,128)(2,1)S(1)} %add_convert_fusion.20.total_ref), channel_id=1, source_target_pairs={{0,8},{8,0},{16,24},{24,16},{1,9},{9,1},{17,25},{25,17},{2,10},{10... | collective-permute-start | bytes 331784 | tf_op jit(solution)/shard_map/ppermute | solution.py:486
  118.2 9.8 %collective-permute-start.45 = (bf16[48,2304]{1,0:T(8,128)(2,1)S(1)}, bf16[48,2304]{1,0:T(8,128)(2,1)S(1)}, u32[]{:S(2)}, u32[]{:S(2)}) collective-permute-start(bf16[48,2304]{1,0:T(8,128)(2,1)S(1)} %select_convert_fusion), channel_id=1, source_target_pairs={{0,8},{8,0},{16,24},{24,16},{1,9},{9,1},{17,25},{25,17},{2,10},{10... | collective-permute-start | bytes 663560 | tf_op jit(solution)/shard_map/ppermute | solution.py:486
  119.7 9.6 %collective-permute-start.38 = (bf16[48,1536]{1,0:T(8,128)(2,1)S(1)}, bf16[48,1536]{1,0:T(8,128)(2,1)S(1)}, u32[]{:S(2)}, u32[]{:S(2)}) collective-permute-start(bf16[48,1536]{1,0:T(8,128)(2,1)S(1)} %get-tuple-element.125), channel_id=1, source_target_pairs={{0,2},{1,3},{2,0},{3,1},{4,6},{5,7},{6,4},{7,5},{8,10},{9,11},{10,... | collective-permute-start | bytes 442376 | tf_op jit(solution)/shard_map/ppermute | solution.py:58
  129.4 23.8 %collective-permute-start.46 = (bf16[48,2304]{1,0:T(8,128)(2,1)S(1)}, bf16[48,2304]{1,0:T(8,128)(2,1)S(1)}, u32[]{:S(2)}, u32[]{:S(2)}) collective-permute-start(bf16[48,2304]{1,0:T(8,128)(2,1)S(1)} %add_convert_fusion.7), channel_id=1, source_target_pairs={{0,16},{8,24},{16,0},{24,8},{1,17},{9,25},{17,1},{25,9},{2,18},{10... | collective-permute-start | bytes 663560 | tf_op jit(solution)/shard_map/ppermute | solution.py:486
  139.4 11.6 %collective-permute-start.41 = (bf16[48,1536]{1,0:T(8,128)(2,1)S(1)}, bf16[48,1536]{1,0:T(8,128)(2,1)S(1)}, u32[]{:S(2)}, u32[]{:S(2)}) collective-permute-start(bf16[48,1536]{1,0:T(8,128)(2,1)S(1)} %add_convert_fusion.13), channel_id=1, source_target_pairs={{0,16},{8,24},{16,0},{24,8},{1,17},{9,25},{17,1},{25,9},{2,18},{10... | collective-permute-start | bytes 442376 | tf_op jit(solution)/shard_map/ppermute | solution.py:486
  153.3 10.0 %collective-permute-start.47 = (bf16[48,2304]{1,0:T(8,128)(2,1)S(1)}, bf16[48,2304]{1,0:T(8,128)(2,1)S(1)}, u32[]{:S(2)}, u32[]{:S(2)}) collective-permute-start(bf16[48,2304]{1,0:T(8,128)(2,1)S(1)} %add_convert_fusion.6.total_ref), channel_id=1, source_target_pairs={{0,8},{8,0},{16,24},{24,16},{1,9},{9,1},{17,25},{25,17},{2,10},{10... | collective-permute-start | bytes 663560 | tf_op jit(solution)/shard_map/ppermute | solution.py:486
  (58 other events, 395.4 us)
